TPU v7x, 32 devices: a whole 2x2x4 slice. The times are simulated.
32 devices in a mesh: seq: 16 (over z, y, x), head: 2 (over core).
Axes of the slice: x: 2, y: 2, z: 4, core: 2. Of those that a mesh axis runs over, the one named last changes fastest.
Arguments:
- x_in: bfloat16 [4096, 2048], P('seq', 'head'), may hold values from -45 to 45
- gate_in: bfloat16 [4096, 2048], P('seq', 'head'), may hold values from -6 to 6
- b_in: bfloat16 [4096, 128], P('seq'), may hold values from -0.375 to 0.375
- c_in: bfloat16 [4096, 128], P('seq'), may hold values from -0.375 to 0.375
- decay_fwd: float32 [32, 4096], P('head', 'seq'), may hold values from -1 to 0
- decay_bwd: float32 [32, 4096], P('head', 'seq'), may hold values from -1 to 0
- skip_gain: float32 [32], P('head'), may hold values from 0.5 to 1.5
- norm_gain: float32 [2048], P('head'), may hold values from 0.1 to 1.9
- w_out: bfloat16 [2048, 1024], P('head'), may hold values from -0.125 to 0.125
- d_out: bfloat16 [4096, 1024], P('seq'), may hold values from -6 to 6
Outputs:
- grad_x: bfloat16 [4096, 2048], P('seq', 'head')
- grad_z: bfloat16 [4096, 2048], P('seq', 'head')
- grad_b: float32 [4096, 128], P('seq')
- grad_c: float32 [4096, 128], P('seq')
- grad_w: float32 [2048, 1024], P('head')
All inputs are finite; a program needn't handle non-finite values.
Results may differ from a plain program's by a relative error of at most 0.0029.
Values sent between devices are 32-bit elements; how exact they have to be, the bound alone decides.
A program may use at most 64 MiB of HBM per device.

v0:
```python
import jax
import jax.numpy as jnp
from jax import lax
from jax.sharding import PartitionSpec as P

HEAD_DIM = 64
INNER = 2048


exact_mode = lax.Precision.HIGHEST
eps_norm = 1e-05
weight_scale = 0.0078125


def prefix(shard, axis, combine, identity, reverse):
    devices, index = (lax.axis_size(axis), lax.axis_index(axis))
    everything = jax.tree.map(lambda part: lax.all_gather(part, axis), shard)
    start = jax.tree.map(
        lambda part, zero: jnp.broadcast_to(jnp.asarray(zero, part.dtype), part.shape),
        shard,
        identity,
    )

    def step(k, before):
        at = devices - 1 - k if reverse else k
        reached = at > index if reverse else at < index
        new = combine(before, jax.tree.map(lambda part: part[at], everything))
        return jax.tree.map(lambda a, b: jnp.where(reached, a, b), new, before)

    return lax.fori_loop(0, devices, step, start)


def link_states(earlier, after_one):
    return (after_one[0] + after_one[1][:, None, None] * earlier[0], earlier[1] * after_one[1])


def carry_up(local_state, decay_total):
    identity = (jnp.zeros_like(local_state), jnp.ones_like(decay_total))
    return prefix((local_state, decay_total), "seq", link_states, identity, False)[0]


def carry_down(local_state, decay_total):
    identity = (jnp.zeros_like(local_state), jnp.ones_like(decay_total))
    return prefix((local_state, decay_total), "seq", link_states, identity, True)[0]


def body(x_in, gate_in, b_in, c_in, decay_fwd, decay_bwd, skip_gain, norm_gain, w_out, d_out):
    frames = x_in.shape[0]
    head_count = decay_fwd.shape[0]
    signal = x_in.astype(jnp.float32).reshape(frames, head_count, HEAD_DIM)
    b_rows = b_in.astype(jnp.float32)
    c_rows = c_in.astype(jnp.float32)
    fwd_cumul = jnp.cumsum(decay_fwd, axis=1)
    bwd_cumul = jnp.cumsum(decay_bwd, axis=1)
    bwd_excl = bwd_cumul - decay_bwd
    fwd_end = fwd_cumul[:, -1:]
    bwd_end = bwd_cumul[:, -1:]
    positions = jnp.arange(frames)
    causal_mask = positions[:, None] >= positions[None, :]
    anti_mask = positions[:, None] <= positions[None, :]
    weights = jnp.exp(
        jnp.where(causal_mask[None], fwd_cumul[:, :, None] - fwd_cumul[:, None, :], -jnp.inf)
    )
    weights = weights + jnp.exp(
        jnp.where(anti_mask[None], bwd_excl[:, None, :] - bwd_excl[:, :, None], -jnp.inf)
    )
    scores = jnp.dot(c_rows, b_rows.T, precision=exact_mode)
    pair_weights = weights * scores[None]
    within = jnp.einsum("hts,shp->thp", pair_weights, signal, precision=exact_mode)
    tail_f = jnp.exp(fwd_end - fwd_cumul)
    lead_b = jnp.exp(bwd_excl)
    rise_f = jnp.exp(fwd_cumul)
    rise_b = jnp.exp(bwd_end - bwd_excl)
    state_f = jnp.einsum("hs,shp,sn->hpn", tail_f, signal, b_rows, precision=exact_mode)
    state_b = jnp.einsum("hs,shp,sn->hpn", lead_b, signal, b_rows, precision=exact_mode)
    decay_f = jnp.exp(fwd_end[:, 0])
    decay_b = jnp.exp(bwd_end[:, 0])
    entry_f = carry_up(state_f, decay_f)
    entry_b = carry_down(state_b, decay_b)
    across = jnp.einsum("tn,hpn,ht->thp", c_rows, entry_f, rise_f, precision=exact_mode)
    across = across + jnp.einsum("tn,hpn,ht->thp", c_rows, entry_b, rise_b, precision=exact_mode)
    merged = (within + across + skip_gain[None, :, None] * signal).reshape(
        frames, head_count * HEAD_DIM
    )
    gate_rows = gate_in.astype(jnp.float32)
    sigmoid_z = jax.nn.sigmoid(gate_rows)
    gated_y = merged * gate_rows * sigmoid_z
    grad_n = lax.dot_general(
        d_out, w_out, (((1,), (1,)), ((), ())), preferred_element_type=jnp.float32
    )
    scaled = grad_n * norm_gain
    square_sum, cross_sum = lax.psum(
        (jnp.sum(gated_y * gated_y, axis=1), jnp.sum(gated_y * scaled, axis=1)), "head"
    )
    inv_rms = lax.rsqrt(square_sum / INNER + eps_norm)[:, None]
    normed = gated_y * inv_rms * norm_gain
    local_w = lax.dot_general(
        normed.astype(jnp.bfloat16),
        d_out,
        (((0,), (0,)), ((), ())),
        preferred_element_type=jnp.float32,
    )
    grad_g = inv_rms * scaled - gated_y * inv_rms * inv_rms * inv_rms * (cross_sum / INNER)[:, None]
    grad_y = grad_g * gate_rows * sigmoid_z
    grad_z = grad_g * merged * sigmoid_z * (1.0 + gate_rows * (1.0 - sigmoid_z))
    grad_rows = grad_y.reshape(frames, head_count, HEAD_DIM)
    back_f_local = jnp.einsum("ht,thp,tn->hpn", rise_f, grad_rows, c_rows, precision=exact_mode)
    back_b_local = jnp.einsum("ht,thp,tn->hpn", rise_b, grad_rows, c_rows, precision=exact_mode)
    dot_pairs = jnp.einsum("thp,shp->hts", grad_rows, signal, precision=exact_mode)
    pair_sum = jnp.sum(weights * dot_pairs, axis=0)
    grad_c_near = jnp.dot(pair_sum, b_rows, precision=exact_mode)
    grad_b_near = jnp.dot(pair_sum.T, c_rows, precision=exact_mode)
    exit_f = carry_down(back_f_local, decay_f)
    exit_b = carry_up(back_b_local, decay_b)
    grad_sig = jnp.einsum("hts,thp->shp", pair_weights, grad_rows, precision=exact_mode)
    grad_sig = grad_sig + jnp.einsum("hpn,sn,hs->shp", exit_f, b_rows, tail_f, precision=exact_mode)
    grad_sig = grad_sig + jnp.einsum("hpn,sn,hs->shp", exit_b, b_rows, lead_b, precision=exact_mode)
    grad_x = (grad_sig + skip_gain[None, :, None] * grad_rows).reshape(
        frames, head_count * HEAD_DIM
    )
    grad_b_far = jnp.einsum("hs,shp,hpn->sn", tail_f, signal, exit_f, precision=exact_mode)
    grad_b_far = grad_b_far + jnp.einsum(
        "hs,shp,hpn->sn", lead_b, signal, exit_b, precision=exact_mode
    )
    grad_c_far = jnp.einsum("ht,thp,hpn->tn", rise_f, grad_rows, entry_f, precision=exact_mode)
    grad_c_far = grad_c_far + jnp.einsum(
        "ht,thp,hpn->tn", rise_b, grad_rows, entry_b, precision=exact_mode
    )
    grad_b, grad_c = lax.psum((grad_b_near + grad_b_far, grad_c_near + grad_c_far), "head")
    grad_w = lax.psum(local_w, "seq") * weight_scale
    return (grad_x.astype(jnp.bfloat16), grad_z.astype(jnp.bfloat16), grad_b, grad_c, grad_w)


def solution(mesh):
    in_specs = (
        P("seq", "head"),
        P("seq", "head"),
        P("seq", None),
        P("seq", None),
        P("head", "seq"),
        P("head", "seq"),
        P("head"),
        P("head"),
        P("head", None),
        P("seq", None),
    )
    out_specs = (
        P("seq", "head"),
        P("seq", "head"),
        P("seq", None),
        P("seq", None),
        P("head", None),
    )
    return jax.shard_map(body, mesh=mesh, in_specs=in_specs, out_specs=out_specs, check_vma=False)
```

profile of v0, /device:TPU:0, one launch (start us, length us, event | category | flops | bytes accessed | tf_op | source)
XLA Modules:
  0.0 751.0 jit_solution(712898297794028119)
XLA Ops:
  15.5 2.3 fusion.43
  19.7 44.4 %all-reduce.2 = (f32[256]{0:T(256)S(1)}, f32[256]{0:T(256)S(1)}) all-reduce(f32[256]{0:T(256)S(1)} %dynamic-update-slice.1, f32[256]{0:T(256)S(1)} %dynamic-update-slice), channel_id=5, replica_groups=mesh['seq'=16,'head'=2] {'seq'}, use_global_device_ids=true, to_apply=%add.1 | all-reduce | flops 512 | bytes 4096
  65.2 5.8 fusion.25
  71.1 58.6 %all-gather.13.cloned.1.call-done = f32[256,64,128]{2,1,0:T(8,128)} async-done(((f32[16,64,128]{2,1,0:T(8,128)}), f32[256,64,128]{2,1,0:T(8,128)}) %all-gather.13.cloned.1.call-update) | async-done | bytes 8388624 | tf_op jit(solution)/shard_map/all_gather | solution.py:17
  129.7 19.6 %while.61 = (s32[]{:T(128)}, f32[16,64,128]{2,1,0:T(8,128)S(1)}, s32[]{:T(128)}, f32[16,16,64,128]{3,2,1,0:T(8,128)}, f32[16,16]{1,0:T(8,128)S(1)}, /*index=5*/s32[]{:T(128)}, s32[]{:T(128)}, s32[]{:T(128)}, s32[]{:T(128)}) while((s32[]{:T(128)}, f32[16,64,128]{2,1,0:T(8,128)S(1)}, s32[]{:T(128)}, f32[16,16,64,128]{3,2,1,0:T(8,128)}, ...), condition=%wide.region_7.8_spmd.clone, body=%wide.region_6.7_spmd.clone.sunk | while | flops 524296 | bytes 1573231 | solution.py:30
  149.4 94.1 %all-gather.11.cloned.1.call-done = f32[256,64,128]{2,1,0:T(8,128)} async-done(((f32[16,64,128]{2,1,0:T(8,128)}), f32[256,64,128]{2,1,0:T(8,128)}) %all-gather.11.cloned.1.call-update) | async-done | bytes 8388624 | tf_op jit(solution)/shard_map/all_gather | solution.py:17
  243.5 19.5 %while.60 = (s32[]{:T(128)}, f32[16,64,128]{2,1,0:T(8,128)S(1)}, s32[]{:T(128)}, f32[16,16,64,128]{3,2,1,0:T(8,128)}, f32[16,16]{1,0:T(8,128)S(1)}, /*index=5*/s32[]{:T(128)}, s32[]{:T(128)}) while((s32[]{:T(128)}, f32[16,64,128]{2,1,0:T(8,128)S(1)}, s32[]{:T(128)}, f32[16,16,64,128]{3,2,1,0:T(8,128)}, f32[16,16]{1,0:T(8,128)S(1)}, ...), condition=%wide.region_5.6_spmd.clone, body=%wide.region_4.5_spmd.clone.sunk | while | flops 524292 | bytes 1573169 | solution.py:30
  263.7 3.0 fusion.34
  266.7 2.5 copy.49
  269.2 3.3 multiply_reduce_fusion.2
  272.5 2.5 all-reduce.3
  275.0 4.4 fusion.64
  290.0 5.2 multiply_reduce_fusion
  296.1 5.3 fusion.28
  301.4 144.5 %all-reduce.8.cloned.1.call-done = f32[1024,1024]{1,0:T(8,128)} async-done(((f32[1024,1024]{1,0:T(8,128)}), f32[1024,1024]{1,0:T(8,128)}) %all-reduce.8.cloned.1.call-update) | async-done | bytes 4194320 | tf_op jit(solution)/shard_map/psum | solution.py:130
  446.0 5.0 broadcast_multiply_fusion
  451.0 109.8 %all-gather.17.cloned.1.call-done = f32[256,64,128]{2,1,0:T(8,128)} async-done(((f32[16,64,128]{2,1,0:T(8,128)}), f32[256,64,128]{2,1,0:T(8,128)}) %all-gather.17.cloned.1.call-update) | async-done | bytes 8388624 | tf_op jit(solution)/shard_map/all_gather | solution.py:17
  560.8 30.1 %while.63 = (s32[]{:T(128)}, f32[16,64,128]{2,1,0:T(8,128)S(1)}, s32[]{:T(128)}, f32[16,16,64,128]{3,2,1,0:T(8,128)}, f32[16,16]{1,0:T(8,128)}, /*index=5*/s32[]{:T(128)}, s32[]{:T(128)}) while((s32[]{:T(128)}, f32[16,64,128]{2,1,0:T(8,128)S(1)}, s32[]{:T(128)}, f32[16,16,64,128]{3,2,1,0:T(8,128)}, f32[16,16]{1,0:T(8,128)}, ...), condition=%wide.region_15.16_spmd.clone, body=%wide.region_14.15_spmd.clone.sunk | while | flops 524292 | bytes 1573169 | solution.py:30
  590.9 2.5 fusion.46
  595.0 79.8 %all-gather.15.cloned.1.call-done = f32[256,64,128]{2,1,0:T(8,128)} async-done(((f32[16,64,128]{2,1,0:T(8,128)}), f32[256,64,128]{2,1,0:T(8,128)}) %all-gather.15.cloned.1.call-update) | async-done | bytes 8388624 | tf_op jit(solution)/shard_map/all_gather | solution.py:17
  674.9 45.2 %while.62 = (s32[]{:T(128)}, f32[16,64,128]{2,1,0:T(8,128)}, s32[]{:T(128)}, f32[16,16,64,128]{3,2,1,0:T(8,128)}, f32[16,16]{1,0:T(8,128)}, /*index=5*/s32[]{:T(128)}, s32[]{:T(128)}, s32[]{:T(128)}, s32[]{:T(128)}) while((s32[]{:T(128)}, f32[16,64,128]{2,1,0:T(8,128)}, s32[]{:T(128)}, f32[16,16,64,128]{3,2,1,0:T(8,128)}, ...), condition=%wide.region_13.14_spmd.clone, body=%wide.region_12.13_spmd.clone.sunk | while | flops 524296 | bytes 1573231 | solution.py:30
  720.1 3.2 fusion.49
  724.4 3.1 fusion.41
  729.5 11.5 %all-reduce.10.cloned.1.call-done = (f32[256,128]{1,0:T(8,128)}, f32[256,128]{1,0:T(8,128)}) async-done(((f32[256,128]{1,0:T(8,128)}, f32[256,128]{1,0:T(8,128)}), (f32[256,128]{1,0:T(8,128)}, f32[256,128]{1,0:T(8,128)})) %all-reduce.10.cloned.1.call-update) | async-done | bytes 262160 | tf_op jit(solution)/shard_map/psum | solution.py:129
  (247 shorter events, 143.3 us)
Async XLA Ops:
  7.2 262.0 %copy-start = (bf16[1024,1024]{1,0:T(8,128)(2,1)S(1)}, bf16[1024,1024]{1,0:T(8,128)(2,1)}, u32[]{:S(2)}) copy-start(bf16[1024,1024]{1,0:T(8,128)(2,1)} %param.26) | copy-start | bytes 6291460
  7.2 10.8 %copy-start.29 = (u32[32]{0:T(128)S(1)}, u32[32]{0:T(128)}, u32[]{:S(2)}) copy-start(u32[32]{0:T(128)} %constant.157) | copy-start | bytes 388
  7.2 57.1 %copy-start.10 = (bf16[256,128]{1,0:T(8,128)(2,1)S(1)}, bf16[256,128]{1,0:T(8,128)(2,1)}, u32[]{:S(2)}) copy-start(bf16[256,128]{1,0:T(8,128)(2,1)} %param.20) | copy-start | bytes 196612
  7.2 57.1 %copy-start.9 = (bf16[256,128]{1,0:T(8,128)(2,1)S(1)}, bf16[256,128]{1,0:T(8,128)(2,1)}, u32[]{:S(2)}) copy-start(bf16[256,128]{1,0:T(8,128)(2,1)} %param.21) | copy-start | bytes 196612
  7.2 122.5 %all-gather.13.cloned.1.call-start = ((), (), s32[]{:S(2)}) async-start(), calls=%async_computation.2 | async-start | bytes 8912896 | tf_op jit(solution)/shard_map/all_gather | solution.py:17
  8.7 9.3 %copy-start.6 = (bf16[256,1024]{0,1:T(8,128)(2,1)}, bf16[256,1024]{0,1:T(8,128)(2,1)S(1)}, u32[]{:S(2)}) copy-start(bf16[256,1024]{0,1:T(8,128)(2,1)S(1)} %copy.48) | copy-start | bytes 1572868
  11.3 59.8 %copy-start.21 = (f32[16,256]{1,0:T(8,128)}, f32[16,256]{1,0:T(8,128)S(1)}, u32[]{:S(2)}) copy-start(f32[16,256]{1,0:T(8,128)S(1)} %get-tuple-element.606) | copy-start | bytes 49156
  13.6 229.9 %all-gather.11.cloned.1.call-start = ((), (), s32[]{:S(2)}) async-start(), calls=%async_computation.1 | async-start | bytes 8912896 | tf_op jit(solution)/shard_map/all_gather | solution.py:17
  15.2 55.8 %copy-start.23 = (f32[16,256]{1,0:T(8,128)}, f32[16,256]{1,0:T(8,128)S(1)}, u32[]{:S(2)}) copy-start(f32[16,256]{1,0:T(8,128)S(1)} %copy_bitcast_fusion.1) | copy-start | bytes 49156
  15.5 55.5 %copy-start.13 = (f32[256,16]{0,1:T(8,128)}, f32[256,16]{0,1:T(8,128)S(1)}, u32[]{:S(2)}) copy-start(f32[256,16]{0,1:T(8,128)S(1)} %get-tuple-element.610) | copy-start | bytes 49156
  17.9 428.1 %all-reduce.8.cloned.1.call-start = ((), (), s32[]{:S(2)}) async-start(), calls=%async_computation | async-start | bytes 8388608 | tf_op jit(solution)/shard_map/psum | solution.py:130
  64.3 6.7 copy-start.17
  64.3 6.7 copy-start.19
  149.3 114.3 %copy-start.4 = (f32[16,64,128]{2,1,0:T(8,128)}, f32[16,64,128]{2,1,0:T(8,128)S(1)}, u32[]{:S(2)}) copy-start(f32[16,64,128]{2,1,0:T(8,128)S(1)} %get-tuple-element.458) | copy-start | bytes 1572868
  149.4 114.3 %copy-start.26 = (f32[16,16]{1,0:T(8,128)}, f32[16,16]{1,0:T(8,128)S(1)}, u32[]{:S(2)}) copy-start(f32[16,16]{1,0:T(8,128)S(1)} %get-tuple-element.870) | copy-start | bytes 3076
  243.5 20.1 %copy-start.27 = (f32[16]{0:T(128)S(1)}, f32[16]{0:T(128)}, u32[]{:S(2)}) copy-start(f32[16]{0:T(128)} %param.24) | copy-start | bytes 196
  263.0 9.5 %copy-start.2 = (f32[16,64,128]{2,1,0:T(8,128)}, f32[16,64,128]{2,1,0:T(8,128)S(1)}, u32[]{:S(2)}) copy-start(f32[16,64,128]{2,1,0:T(8,128)S(1)} %get-tuple-element.457) | copy-start | bytes 1572868
  263.0 9.5 %copy-start.25 = (f32[16,16]{1,0:T(8,128)}, f32[16,16]{1,0:T(8,128)S(1)}, u32[]{:S(2)}) copy-start(f32[16,16]{1,0:T(8,128)S(1)} %get-tuple-element.869) | copy-start | bytes 3076
  279.4 281.4 %all-gather.17.cloned.1.call-start = ((), (), s32[]{:S(2)}) async-start(), calls=%async_computation.4 | async-start | bytes 8912896 | tf_op jit(solution)/shard_map/all_gather | solution.py:17
  283.1 6.9 copy-start.7
  284.6 390.3 %all-gather.15.cloned.1.call-start = ((), (), s32[]{:S(2)}) async-start(), calls=%async_computation.3 | async-start | bytes 8912896 | tf_op jit(solution)/shard_map/all_gather | solution.py:17
  286.1 455.0 %all-reduce.10.cloned.1.call-start = ((), (), s32[]{:S(2)}) async-start(), calls=%async_computation.5 | async-start | bytes 524288 | tf_op jit(solution)/shard_map/psum | solution.py:129
  595.0 125.1 %copy-start.14 = (f32[256,16]{0,1:T(8,128)S(1)}, f32[256,16]{0,1:T(8,128)}, u32[]{:S(2)}) copy-start(f32[256,16]{0,1:T(8,128)} %copy-done.13) | copy-start | bytes 49156
  720.1 24.1 %copy-start.1 = (bf16[1024,1024]{1,0:T(8,128)(2,1)S(1)}, bf16[1024,1024]{1,0:T(8,128)(2,1)}, u32[]{:S(2)}) copy-start(bf16[1024,1024]{1,0:T(8,128)(2,1)} %param.26) | copy-start | bytes 6291460
  (12 other events, 63.8 us)
Sparse Core Ops, SparseCore 0:
  13.7 115.9 all-gather.12
  132.5 111.0 all-gather.10
  279.6 166.3 all-reduce.7
  449.0 111.7 all-gather.16
  563.8 111.0 all-gather.14
  724.5 16.4 all-reduce.9
where the time goes:
time: 755 us; the launch traced here: 751 us
  waiting for transfers between devices  499 us (66%)
  other arithmetic  100 us (13%)
  matrix products  51.2 us (7%)
  blocking collectives  46.9 us (6%)
  local copies, waits for them, and re-layouts  37 us (5%)
  between operations  15.3 us (2%)
    all_gather x4, waiting for transfers between devices, prefix(): everything = jax.tree.map(lambda part: lax.all_gather(part, axis), shard)  342 us
    psum x1, waiting for transfers between devices, body(): grad_w = lax.psum(local_w, 'seq') * weight_scale  145 us
    select_n x64, other arithmetic, step(): return jax.tree.map(lambda a, b: jnp.where(reached, a, b), new, before)  91 us
    unnamed x1, blocking collectives  44.4 us
    mul x64, local copies, waits for them, and re-layouts, link_states(): after_one[1][:, None, None] * earlier[0]  22 us
  transfers between devices with their start and end apart: 6, of which 6 were waited for; matrix products, arithmetic and copies ran while one was open for 13% of the time, Pallas kernels for 0%

commit v1 on v0

v1 whole, which is shorter than its diff:
```python
import functools

import jax
import jax.numpy as jnp
from jax import lax
from jax.experimental import pallas as pl
from jax.experimental.pallas import tpu as pltpu
from jax.sharding import PartitionSpec as P

HEAD_DIM = 64
PAIR = 2 * HEAD_DIM
QUAD = 4
F32 = jnp.float32
BF16 = jnp.bfloat16
eps_norm = 1e-05
weight_scale = 0.0078125
VMEM_BYTES = 48 * 1024 * 1024


def dot(a, b, ca, cb):
    return lax.dot_general(a, b, (((ca,), (cb,)), ((), ())), preferred_element_type=F32)


def split(a):
    high = a.astype(BF16)
    return high, (a - high.astype(F32)).astype(BF16)


def dot_split_left(a, b, ca, cb):
    high, low = split(a)
    return dot(high, b, ca, cb) + dot(low, b, ca, cb)


def dot_split_right(a, b, ca, cb):
    high, low = split(b)
    return dot(a, high, ca, cb) + dot(a, low, ca, cb)


def dot_split_both(a, b, ca, cb):
    a_high, a_low = split(a)
    b_high, b_low = split(b)
    return dot(a_high, b_high, ca, cb) + (dot(a_high, b_low, ca, cb) + dot(a_low, b_high, ca, cb))


def by_head(first, second, frames):
    lane = lax.broadcasted_iota(jnp.int32, (frames, PAIR), 1)
    return jnp.where(lane < HEAD_DIM, first, second)


def pair_column(cols, at, frames):
    return by_head(cols[:, at : at + 1], cols[:, 4 + at : 5 + at], frames)


def pair_weights(cols, rows, e, frames, later_rows):
    f_col, b_col = cols[:, 4 * e : 4 * e + 1], cols[:, 4 * e + 1 : 4 * e + 2]
    f_row, b_row = rows[4 * e : 4 * e + 1, :], rows[4 * e + 1 : 4 * e + 2, :]
    i = lax.broadcasted_iota(jnp.int32, (frames, frames), 0)
    j = lax.broadcasted_iota(jnp.int32, (frames, frames), 1)
    if later_rows:
        power = jnp.where(i >= j, f_col - f_row, b_row - b_col)
    else:
        power = jnp.where(j >= i, f_row - f_col, b_col - b_row)
    weight = jnp.exp(power)
    return jnp.where(i == j, 2.0 * weight, weight)


def state_kernel(x_ref, b_ref, cols_ref, out_ref):
    frames = x_ref.shape[0]
    cols = cols_ref[0]
    x = x_ref[...].astype(F32)
    tail = jnp.exp(pair_column(cols, 2, frames))
    lead = jnp.exp(pair_column(cols, 1, frames))
    out_ref[0] = dot_split_left(x * tail, b_ref[...], 0, 0)
    out_ref[1] = dot_split_left(x * lead, b_ref[...], 0, 0)


def within_kernel(x_ref, b_ref, c_ref, cols_ref, rows_ref, w_ref, d_ref, gain_ref, skip_ref,
                  y_ref, m_ref, scores):
    frames = x_ref.shape[0]

    @pl.when(pl.program_id(0) == 0)
    def _():
        scores[...] = dot(c_ref[...], b_ref[...], 1, 1)

    cols, rows = cols_ref[0], rows_ref[0]
    x = x_ref[...]
    parts = []
    for e in range(2):
        pw = pair_weights(cols, rows, e, frames, True) * scores[...]
        parts.append(dot_split_left(pw, x, 1, 0))
    y_ref[...] = by_head(parts[0], parts[1], frames) + skip_ref[...] * x.astype(F32)
    m_ref[...] = dot(d_ref[...], w_ref[...], 1, 1) * gain_ref[...]


def merge_kernel(near_ref, m_ref, z_ref, c_ref, cols_ref, entry_ref, y_ref, sums_ref, sq, cross):
    frames = near_ref.shape[0]
    step = pl.program_id(0)

    @pl.when(step == 0)
    def _():
        sq[...] = jnp.zeros_like(sq)
        cross[...] = jnp.zeros_like(cross)

    cols = cols_ref[0]
    c = c_ref[...]
    y = near_ref[...]
    y = y + jnp.exp(pair_column(cols, 0, frames)) * dot_split_right(c, entry_ref[0], 1, 1)
    y = y + jnp.exp(pair_column(cols, 3, frames)) * dot_split_right(c, entry_ref[1], 1, 1)
    y_ref[...] = y
    z = z_ref[...].astype(F32)
    u = y * z * (1.0 / (1.0 + jnp.exp(-z)))
    sq[...] += u * u
    cross[...] += u * m_ref[...]

    @pl.when(step == pl.num_programs(0) - 1)
    def _():
        sums_ref[:, 0:1] = jnp.sum(sq[...], axis=1, keepdims=True)
        sums_ref[:, 1:2] = jnp.sum(cross[...], axis=1, keepdims=True)


def turn_kernel(inner, y_ref, m_ref, z_ref, c_ref, cols_ref, sums_ref, gain_ref, d_ref,
                dy_ref, gz_ref, back_ref, *w_refs):
    frames = y_ref.shape[0]
    cols = cols_ref[0]
    y = y_ref[...]
    z = z_ref[...].astype(F32)
    sig = 1.0 / (1.0 + jnp.exp(-z))
    silu = z * sig
    u = y * silu
    q = lax.rsqrt(sums_ref[:, 0:1] * (1.0 / inner) + eps_norm)
    k = sums_ref[:, 1:2] * (1.0 / inner)
    du = q * m_ref[...] - u * (q * q * q * k)
    dy = du * silu
    dy_ref[...] = dy
    gz_ref[...] = (du * y * sig * (1.0 + z * (1.0 - sig))).astype(BF16)
    n = (u * q * gain_ref[...]).astype(BF16)
    c = c_ref[...]
    back_ref[0] = dot_split_left(dy * jnp.exp(pair_column(cols, 0, frames)), c, 0, 0)
    back_ref[1] = dot_split_left(dy * jnp.exp(pair_column(cols, 3, frames)), c, 0, 0)
    at = 0
    for w_ref in w_refs:
        columns = w_ref.shape[1]
        w_ref[...] = dot(n, d_ref[:, at : at + columns], 0, 0) * weight_scale
        at += columns


def near_kernel(x_ref, b_ref, c_ref, cols_ref, rows_ref, skip_ref, dy_ref, entry_ref,
                gx_ref, gb_ref, gc_ref, scores, pairs):
    frames = x_ref.shape[0]
    step = pl.program_id(0)

    @pl.when(step == 0)
    def _():
        scores[...] = dot(b_ref[...], c_ref[...], 1, 1)
        pairs[...] = jnp.zeros_like(pairs)
        gc_ref[...] = jnp.zeros_like(gc_ref)

    cols, rows = cols_ref[0], rows_ref[0]
    x = x_ref[...]
    dy = dy_ref[...]
    lane = lax.broadcasted_iota(jnp.int32, (frames, PAIR), 1)
    parts = []
    for e in range(2):
        weight = pair_weights(cols, rows, e, frames, False)
        own = (lane < HEAD_DIM) if e == 0 else (lane >= HEAD_DIM)
        dy_own = jnp.where(own, dy, 0.0)
        pairs[...] += weight * dot_split_right(x, dy_own, 1, 1)
        parts.append(dot_split_both(weight * scores[...], dy_own, 1, 0))
    gx_ref[...] = parts[0] + parts[1] + skip_ref[...] * dy
    gc_ref[...] += dot_split_both(dy * jnp.exp(pair_column(cols, 0, frames)), entry_ref[0], 1, 0)
    gc_ref[...] += dot_split_both(dy * jnp.exp(pair_column(cols, 3, frames)), entry_ref[1], 1, 0)

    @pl.when(step == pl.num_programs(0) - 1)
    def _():
        gb_ref[...] = dot_split_left(pairs[...], c_ref[...], 1, 0)
        gc_ref[...] += dot_split_left(pairs[...], b_ref[...], 0, 0)


def far_kernel(x_ref, b_ref, cols_ref, exit_ref, near_ref, gb_near_ref, gx_ref, gb_ref):
    frames = x_ref.shape[0]

    @pl.when(pl.program_id(0) == 0)
    def _():
        gb_ref[...] = gb_near_ref[...]

    cols = cols_ref[0]
    b = b_ref[...]
    x = x_ref[...].astype(F32)
    tail = jnp.exp(pair_column(cols, 2, frames))
    lead = jnp.exp(pair_column(cols, 1, frames))
    far = tail * dot_split_right(b, exit_ref[0], 1, 1) + lead * dot_split_right(b, exit_ref[1], 1, 1)
    gx_ref[...] = (near_ref[...] + far).astype(BF16)
    gb_ref[...] += dot_split_both(x * tail, exit_ref[0], 1, 0)
    gb_ref[...] += dot_split_both(x * lead, exit_ref[1], 1, 0)


def call(kernel, name, grid, ins, in_specs, outs, out_specs, scratch=(), flops=0):
    moved = sum(a.size * a.dtype.itemsize for a in ins) + sum(
        o.size * o.dtype.itemsize for o in outs)
    return pl.pallas_call(
        kernel,
        name=name,
        grid=(grid,),
        in_specs=in_specs,
        out_specs=out_specs,
        out_shape=outs,
        scratch_shapes=list(scratch),
        compiler_params=pltpu.CompilerParams(
            dimension_semantics=("arbitrary",), vmem_limit_bytes=VMEM_BYTES),
        cost_estimate=pl.CostEstimate(flops=flops, bytes_accessed=moved, transcendentals=0),
    )(*ins)


def sum_over(value, axis):
    size = lax.axis_size(axis)
    reach = 1
    while reach < size:
        value = value + lax.ppermute(value, axis, [(i, i ^ reach) for i in range(size)])
        reach *= 2
    return value


def sum_slabs(value, bits):
    size, me = lax.axis_size("seq"), lax.axis_index("seq")
    for bit in bits:
        mine = (me >> bit) & 1
        halves = value.reshape(2, value.shape[0] // 2, value.shape[1])
        sent = lax.dynamic_index_in_dim(halves, 1 - mine, 0, keepdims=False)
        came = lax.ppermute(sent, "seq", [(i, i ^ (1 << bit)) for i in range(size)])
        value = lax.dynamic_index_in_dim(halves, mine, 0, keepdims=False) + came
    for bit in reversed(bits):
        mine = (me >> bit) & 1
        came = lax.ppermute(value, "seq", [(i, i ^ (1 << bit)) for i in range(size)])
        first = jnp.where(mine == 0, value, came)
        second = jnp.where(mine == 0, came, value)
        value = jnp.concatenate([first, second], axis=0)
    return value


def carry(up, up_logs, down, down_logs):
    size, me = lax.axis_size("seq"), lax.axis_index("seq")
    groups = size // QUAD
    q, g = me % QUAD, me // QUAD
    rows, width = up.shape
    heads = up_logs.shape[1]
    part, part_heads = rows // QUAD, heads // QUAD
    both = jnp.stack([up, down]).reshape(2, QUAD, part, width)

    def block(r):
        return lax.dynamic_index_in_dim(both, q ^ r, 1, keepdims=False)

    held = [block(0)] + [
        lax.ppermute(block(r), "seq", [(i, i ^ r) for i in range(size)]) for r in range(1, QUAD)]

    def my_logs(logs):
        mine = lax.dynamic_slice_in_dim(logs, q * part_heads, part_heads, 1)
        return mine.reshape(groups, QUAD, part_heads)

    def scale(logs, state):
        factor = jnp.exp(logs)[:, None, None]
        return (factor * state.reshape(part_heads, -1, width)).reshape(part, width)

    answers = []
    for k, logs in ((0, my_logs(up_logs)), (1, my_logs(down_logs))):
        rising = k == 0

        def ahead(a, b):
            return (a > b) if rising else (a < b)

        own = lax.dynamic_index_in_dim(logs, g, 0, keepdims=False)
        place = jnp.arange(QUAD)
        group_logs = jnp.sum(logs, axis=1)

        def between(low, high):
            keep = jnp.ones((QUAD,), bool)
            if low is not None:
                keep = keep & ahead(place, low)
            if high is not None:
                keep = keep & ahead(high, place)
            return jnp.sum(jnp.where(keep[:, None], own, 0.0), axis=0)

        states = [held[r][k] for r in range(QUAD)]
        total = sum(scale(between(q ^ r, None), states[r]) for r in range(QUAD))
        group_place = jnp.arange(groups)
        sign = 1 if rising else -1
        whole = lax.dynamic_index_in_dim(group_logs, g, 0, keepdims=False)
        entering = None
        reach = 1
        while reach < groups:
            sent = total if entering is None else total + scale(whole, entering)
            moves = [(i, i + sign * reach * QUAD) for i in range(size)
                     if 0 <= i + sign * reach * QUAD < size]
            came = lax.ppermute(sent, "seq", moves)
            if entering is None:
                entering = came
            else:
                steps = (g - group_place) * sign
                keep = (steps >= 1) & (steps < reach)
                passed = jnp.sum(jnp.where(keep[:, None], group_logs, 0.0), axis=0)
                entering = entering + scale(passed, came)
            reach *= 2
        replies = []
        for r in range(QUAD):
            reply = scale(between(None, q ^ r), entering)
            for s in range(QUAD):
                if s != r:
                    term = scale(between(q ^ s, q ^ r), states[s])
                    reply = reply + jnp.where(ahead(q ^ r, q ^ s), term, 0.0)
            replies.append(reply)
        answers.append(replies)
    full = jnp.zeros((2, QUAD, part, width), F32)
    for r in range(QUAD):
        reply = jnp.stack([answers[0][r], answers[1][r]])
        if r:
            reply = lax.ppermute(reply, "seq", [(i, i ^ r) for i in range(size)])
        full = lax.dynamic_update_slice_in_dim(full, reply[:, None], q ^ r, 1)
    return full.reshape(2, rows, width)


def body(x_in, gate_in, b_in, c_in, decay_fwd, decay_bwd, skip_gain, norm_gain, w_out, d_out):
    frames, width = x_in.shape
    heads = decay_fwd.shape[0]
    state = b_in.shape[1]
    model = d_out.shape[1]
    pairs = heads // 2
    inner = width * lax.axis_size("head")

    fwd = jnp.cumsum(decay_fwd, axis=1)
    bwd = jnp.cumsum(decay_bwd, axis=1) - decay_bwd
    fwd_end = fwd[:, -1:]
    bwd_end = bwd[:, -1:] + decay_bwd[:, -1:]
    lines = jnp.stack([fwd, bwd, fwd_end - fwd, bwd_end - bwd], axis=1)
    rows = lines.reshape(pairs, 8, frames)
    cols = rows.transpose(0, 2, 1)
    ends = lax.all_gather(jnp.stack([fwd_end[:, 0], bwd_end[:, 0]]), "seq")
    logs_f, logs_b = ends[:, 0], ends[:, 1]
    skip = jnp.repeat(skip_gain, HEAD_DIM)[None, :]
    gain = norm_gain[None, :]

    wide = pl.BlockSpec((frames, PAIR), lambda i: (0, i))
    narrow = pl.BlockSpec((frames, state), lambda i: (0, 0))
    col = pl.BlockSpec((1, frames, 8), lambda i: (i, 0, 0))
    row = pl.BlockSpec((1, 8, frames), lambda i: (i, 0, 0))
    lanes = pl.BlockSpec((1, PAIR), lambda i: (0, i))
    states = pl.BlockSpec((2, PAIR, state), lambda i: (0, i, 0))
    model_rows = pl.BlockSpec((frames, model), lambda i: (0, 0))
    weight_rows = pl.BlockSpec((PAIR, model), lambda i: (i, 0))
    sums_spec = pl.BlockSpec((frames, 2), lambda i: (0, 0))
    shape = jax.ShapeDtypeStruct
    wide_f32, wide_bf16 = shape((frames, width), F32), shape((frames, width), BF16)
    state_out, narrow_out = shape((2, width, state), F32), shape((frames, state), F32)
    square = pltpu.VMEM((frames, frames), F32)
    lane_sums = pltpu.VMEM((frames, PAIR), F32)
    quad_flops = 2 * frames * frames * width

    local = call(state_kernel, "local_states", pairs, (x_in, b_in, cols), [wide, narrow, col],
                 [state_out], [states], flops=8 * frames * width * state)[0]
    entry = carry(local[0], logs_f, local[1], logs_b)
    near_y, scaled = call(
        within_kernel, "within_slab", pairs,
        (x_in, b_in, c_in, cols, rows, w_out, d_out, gain, skip),
        [wide, narrow, narrow, col, row, weight_rows, model_rows, lanes, lanes],
        [wide_f32, wide_f32], [wide, wide], [square],
        flops=8 * quad_flops + 2 * frames * width * model)
    y, sums = call(
        merge_kernel, "merge_entry", pairs, (near_y, scaled, gate_in, c_in, cols, entry),
        [wide, wide, wide, narrow, col, states],
        [wide_f32, shape((frames, 2), F32)], [wide, sums_spec], [lane_sums, lane_sums],
        flops=8 * frames * width * state)
    sums = sum_over(sums, "head")
    bits = list(range((lax.axis_size("seq") - 1).bit_length()))
    orders = (bits, [bits[1], bits[0]] + bits[2:], bits[2:] + bits[:2])
    thirds = model // 8 * 3
    chunks = (thirds, thirds, model - 2 * thirds)
    dy, grad_z, back, *local_w = call(
        functools.partial(turn_kernel, inner), "norm_backward", pairs,
        (y, scaled, gate_in, c_in, cols, sums, gain, d_out),
        [wide, wide, wide, narrow, col, sums_spec, lanes, model_rows],
        [wide_f32, wide_bf16, state_out] + [shape((width, n), F32) for n in chunks],
        [wide, wide, states] + [pl.BlockSpec((PAIR, n), lambda i: (i, 0)) for n in chunks],
        flops=2 * frames * width * model + 8 * frames * width * state)
    exits = carry(back[1], logs_b, back[0], logs_f)
    grad_w = jnp.concatenate(
        [sum_slabs(part, order) for part, order in zip(local_w, orders)], axis=1)
    near_x, near_b, grad_c = call(
        near_kernel, "near_gradients", pairs,
        (x_in, b_in, c_in, cols, rows, skip, dy, entry),
        [wide, narrow, narrow, col, row, lanes, wide, states],
        [wide_f32, narrow_out, narrow_out], [wide, narrow, narrow], [square, square],
        flops=20 * quad_flops)
    grad_c = sum_over(grad_c, "head")
    exits = jnp.stack([exits[1], exits[0]])
    grad_x, grad_b = call(
        far_kernel, "far_gradients", pairs, (x_in, b_in, cols, exits, near_x, near_b),
        [wide, narrow, col, states, wide, narrow],
        [wide_bf16, narrow_out], [wide, narrow], flops=20 * frames * width * state)
    grad_b = sum_over(grad_b, "head")
    return grad_x, grad_z, grad_b, grad_c, grad_w


def solution(mesh):
    in_specs = (
        P("seq", "head"),
        P("seq", "head"),
        P("seq", None),
        P("seq", None),
        P("head", "seq"),
        P("head", "seq"),
        P("head"),
        P("head"),
        P("head", None),
        P("seq", None),
    )
    out_specs = (
        P("seq", "head"),
        P("seq", "head"),
        P("seq", None),
        P("seq", None),
        P("head", None),
    )
    return jax.shard_map(body, mesh=mesh, in_specs=in_specs, out_specs=out_specs, check_vma=False)
```

time: 755 us -> 376 us (0.50)
  waiting for transfers between devices: 499 us -> 120 us
  other arithmetic: 100 us -> 24.1 us
  local copies, waits for them, and re-layouts: 37 us -> 109 us
  matrix products: 51.2 us -> 0 us
  starting transfers between devices: 0.43 us -> 40.9 us
  Pallas kernels: 0 us -> 35.5 us
  between operations: 15.3 us -> 3.05 us
    all_gather x4 -> x0, waiting for transfers between devices: 342 us -> none  [prefix(): everything = jax.tree.map(lambda part: lax.all_gather(part, axis), shard)]
    psum x2 -> x0, waiting for transfers between devices: 156 us -> none  [the longest x1 145 us: body(): grad_w = lax.psum(local_w, 'seq') * weight_scale]
    ppermute x0 -> x47, waiting for transfers between devices: none -> 120 us  [the longest x8 35.2 us: carry(): came = lax.ppermute(sent, 'seq', moves)]
    select_n x64 -> x12, other arithmetic: 91 us -> 0.55 us  [sum_slabs(): first = jnp.where(mine == 0, value, came)]
    dot_general x20 -> x0, matrix products: 51.2 us -> none  [the longest x1 5.81 us: body(): jnp.einsum('hts,shp->thp', pair_weights, signal, precision=exact_mode)]
    unnamed x1 -> x0, blocking collectives: 44.4 us -> none
    all_gather x0 -> x1, blocking collectives: none -> 41.4 us  [body(): ends = lax.all_gather(jnp.stack([fwd_end[:, 0], bwd_end[:, 0]]), 'seq')]
    ppermute x0 -> x47, starting transfers between devices: none -> 40.9 us  [the longest x8 12.3 us: carry(): came = lax.ppermute(sent, 'seq', moves)]
  transfers between devices with their start and end apart: 6 -> 47, of which waited for: 6 -> 30; matrix products, arithmetic and copies ran while one was open for 13% -> 30% of each run, Pallas kernels for 0% -> 5%
where the time goes in v1:
time: 376 us; the launch traced here: 374 us
  waiting for transfers between devices  120 us (32%)
  local copies, waits for them, and re-layouts  109 us (29%)
  blocking collectives  41.4 us (11%)
  starting transfers between devices  40.9 us (11%)
  Pallas kernels  35.5 us (9%)
  other arithmetic  24.1 us (6%)
    mul x172, local copies, waits for them, and re-layouts, scale(): return (factor * state.reshape(part_heads, -1, width)).reshape(part, width)  63.3 us
    all_gather x1, blocking collectives, body(): ends = lax.all_gather(jnp.stack([fwd_end[:, 0], bwd_end[:, 0]]), 'seq')  41.4 us
    pallas_call x6, Pallas kernels, call(): pl.pallas_call(kernel, name=name, grid=(grid,), in_specs=in_specs, out_sp...  35.5 us
    ppermute x8, waiting for transfers between devices, carry(): came = lax.ppermute(sent, 'seq', moves)  35.2 us
    exp x86, local copies, waits for them, and re-layouts, scale(): factor = jnp.exp(logs)[:, None, None]  32 us
    ppermute x12, waiting for transfers between devices, sum_slabs(): came = lax.ppermute(sent, 'seq', [(i, i ^ 1 << bit) for i in range(size)])  30.8 us
    ppermute x12, waiting for transfers between devices, sum_slabs(): came = lax.ppermute(value, 'seq', [(i, i ^ 1 << bit) for i in range(size)])  30.5 us
    ppermute x6, waiting for transfers between devices, carry(): reply = lax.ppermute(reply, 'seq', [(i, i ^ r) for i in range(size)])  19.3 us
  transfers between devices with their start and end apart: 47, of which 30 were waited for; matrix products, arithmetic and copies ran while one was open for 30% of the time, Pallas kernels for 5%

profile of v1, /device:TPU:0, one launch (start us, length us, event | category | flops | bytes accessed | tf_op | source)
XLA Modules:
  0.0 374.1 jit_solution(18334759936182838029)
XLA Ops:
  8.6 4.0 %local_states.1 = f32[2,1024,128]{2,1,0:T(8,128)S(1)} custom-call(bf16[256,1024]{1,0:T(8,128)(2,1)S(1)} %copy-done.7, bf16[256,128]{1,0:T(8,128)(2,1)S(1)} %copy-done.15, f32[8,256,8]{2,1,0:T(8,128)S(1)} %bitcast.336), custom_call_target="tpu_custom_call" | custom-call | flops 268435456 | bytes 1703936 | tf_op jit(solution)/shard_map/local_states/pallas_call | solution.py:200
  13.4 3.9 %collective-permute-start.2 = (f32[2,256,128]{2,1,0:T(8,128)}, f32[2,256,128]{2,1,0:T(8,128)S(1)}, u32[]{:S(2)}, u32[]{:S(2)}) collective-permute-start(f32[2,256,128]{2,1,0:T(8,128)} %get-tuple-element.150), channel_id=1, source_target_pairs={{0,6},{2,4},{4,2},{6,0},{8,14},{10,12},{12,10},{14,8},{16,22},{18,... | collective-permute-start | bytes 786440 | tf_op jit(solution)/shard_map/ppermute | solution.py:253
  22.0 41.4 %all-gather.1 = f32[16,2,16]{2,1,0:T(2,128)S(1)} all-gather(f32[1,2,16]{2,1,0:T(2,128)S(1)} %maximum_bitcast_fusion.2), channel_id=2, replica_groups=mesh['seq'=16,'head'=2] {'seq'}, dimensions={0}, use_global_device_ids=true | all-gather | bytes 2176 | tf_op jit(solution)/shard_map/all_gather | solution.py:335
  151.3 7.6 %within_slab.1 = (f32[256,1024]{1,0:T(8,128)S(1)}, f32[256,1024]{1,0:T(8,128)S(1)}) custom-call(bf16[256,1024]{1,0:T(8,128)(2,1)S(1)} %copy-done.8, bf16[256,128]{1,0:T(8,128)(2,1)S(1)} %copy-done.16, bf16[256,128]{1,0:T(8,128)(2,1)S(1)} %copy-done.14, f32[8,256,8]{2,1,0:T(8,128)S(1)} %bitcast.337, f32[8,8,256]{2,1,0:T(8,128)S(1)} %reshape.868.rows_ref, ...), custom_call_target="tpu_custom_call" | custom-call | flops 1610612736 | bytes 5513216 | tf_op jit(solution)/shard_map/within_slab/pallas_call | solution.py:200
  161.8 4.1 %collective-permute-done.5 = f32[256,128]{1,0:T(8,128)S(1)} collective-permute-done((f32[256,128]{1,0:T(8,128)S(1)}, f32[256,128]{1,0:T(8,128)S(1)}, u32[]{:S(2)}, u32[]{:S(2)}) %collective-permute-start.5) | collective-permute-done | bytes 131104 | tf_op jit(solution)/shard_map/ppermute | solution.py:293
  168.7 5.5 %collective-permute-done.6 = f32[256,128]{1,0:T(8,128)S(1)} collective-permute-done((f32[256,128]{1,0:T(8,128)S(1)}, f32[256,128]{1,0:T(8,128)S(1)}, u32[]{:S(2)}, u32[]{:S(2)}) %collective-permute-start.6) | collective-permute-done | bytes 131104 | tf_op jit(solution)/shard_map/ppermute | solution.py:293
  181.9 4.2 %collective-permute-done.9 = f32[2,256,128]{2,1,0:T(8,128)S(1)} collective-permute-done((f32[2,256,128]{2,1,0:T(8,128)S(1)}, f32[2,256,128]{2,1,0:T(8,128)S(1)}, u32[]{:S(2)}, u32[]{:S(2)}) %collective-permute-start.9) | collective-permute-done | bytes 262176 | tf_op jit(solution)/shard_map/ppermute | solution.py:315
  212.3 9.2 %norm_backward.1 = (f32[256,1024]{1,0:T(8,128)S(1)}, bf16[256,1024]{1,0:T(8,128)(2,1)}, f32[2,1024,128]{2,1,0:T(8,128)S(1)}, f32[1024,384]{1,0:T(8,128)}, f32[1024,384]{1,0:T(8,128)}, /*index=5*/f32[1024,256]{1,0:T(8,128)S(1)}) custom-call(f32[256,1024]{1,0:T(8,128)S(1)} %copy-done.11, f32[256,1024]{1,0:T(8,128)} %copy-done.4, ...), custom_call_target="tpu_custom_call" | custom-call | flops 805306368 | bytes 10098688 | tf_op jit(solution)/shard_map/norm_backward/pallas_call | solution.py:200
  225.4 6.9 %near_gradients.1 = (f32[256,1024]{1,0:T(8,128)S(1)}, f32[256,128]{1,0:T(8,128)S(1)}, f32[256,128]{1,0:T(8,128)S(1)}) custom-call(bf16[256,1024]{1,0:T(8,128)(2,1)S(1)} %copy-done.9, bf16[256,128]{1,0:T(8,128)(2,1)S(1)} %copy-done.16, bf16[256,128]{1,0:T(8,128)(2,1)S(1)} %copy-done.14, f32[8,256,8]{2,1,0:T(8,128)S(1)} %bitcast.340, ...), custom_call_target="tpu_custom_call" | custom-call | flops 2684354560 | bytes 4198400 | tf_op jit(solution)/shard_map/near_gradients/pallas_call | solution.py:200
  232.8 3.7 collective-permute-done.12
  239.0 8.4 %collective-permute-done.14 = f32[256,128]{1,0:T(8,128)S(1)} collective-permute-done((f32[256,128]{1,0:T(8,128)S(1)}, f32[256,128]{1,0:T(8,128)S(1)}, u32[]{:S(2)}, u32[]{:S(2)}) %collective-permute-start.14) | collective-permute-done | bytes 131104 | tf_op jit(solution)/shard_map/ppermute | solution.py:293
  248.8 6.5 %collective-permute-done.16 = f32[256,128]{1,0:T(8,128)S(1)} collective-permute-done((f32[256,128]{1,0:T(8,128)S(1)}, f32[256,128]{1,0:T(8,128)S(1)}, u32[]{:S(2)}, u32[]{:S(2)}) %collective-permute-start.16) | collective-permute-done | bytes 131104 | tf_op jit(solution)/shard_map/ppermute | solution.py:293
  264.3 9.9 %collective-permute-done.17 = f32[256,128]{1,0:T(8,128)S(1)} collective-permute-done((f32[256,128]{1,0:T(8,128)S(1)}, f32[256,128]{1,0:T(8,128)S(1)}, u32[]{:S(2)}, u32[]{:S(2)}) %collective-permute-start.17) | collective-permute-done | bytes 131104 | tf_op jit(solution)/shard_map/ppermute | solution.py:293
  282.0 10.3 %collective-permute-done.19 = f32[2,256,128]{2,1,0:T(8,128)S(1)} collective-permute-done((f32[2,256,128]{2,1,0:T(8,128)S(1)}, f32[2,256,128]{2,1,0:T(8,128)S(1)}, u32[]{:S(2)}, u32[]{:S(2)}) %collective-permute-start.19) | collective-permute-done | bytes 262176 | tf_op jit(solution)/shard_map/ppermute | solution.py:315
  292.5 4.8 %collective-permute-done.41 = f32[128,256]{1,0:T(8,128)S(1)} collective-permute-done((f32[128,256]{1,0:T(8,128)S(1)}, f32[128,256]{1,0:T(8,128)S(1)}, u32[]{:S(2)}, u32[]{:S(2)}) %collective-permute-start.41) | collective-permute-done | bytes 131104 | tf_op jit(solution)/shard_map/ppermute | solution.py:229
  297.7 4.1 %collective-permute-done.42 = f32[64,256]{1,0:T(8,128)S(1)} collective-permute-done((f32[64,256]{1,0:T(8,128)S(1)}, f32[64,256]{1,0:T(8,128)S(1)}, u32[]{:S(2)}, u32[]{:S(2)}) %collective-permute-start.42) | collective-permute-done | bytes 65568 | tf_op jit(solution)/shard_map/ppermute | solution.py:229
  302.9 4.0 %collective-permute-done.43 = f32[64,256]{1,0:T(8,128)S(1)} collective-permute-done((f32[64,256]{1,0:T(8,128)S(1)}, f32[64,256]{1,0:T(8,128)S(1)}, u32[]{:S(2)}, u32[]{:S(2)}) %collective-permute-start.43) | collective-permute-done | bytes 65568 | tf_op jit(solution)/shard_map/ppermute | solution.py:233
  307.8 4.3 %collective-permute-done.44 = f32[128,256]{1,0:T(8,128)S(1)} collective-permute-done((f32[128,256]{1,0:T(8,128)S(1)}, f32[128,256]{1,0:T(8,128)S(1)}, u32[]{:S(2)}, u32[]{:S(2)}) %collective-permute-start.44) | collective-permute-done | bytes 131104 | tf_op jit(solution)/shard_map/ppermute | solution.py:233
  315.2 5.4 %collective-permute-done.33 = f32[128,384]{1,0:T(8,128)S(1)} collective-permute-done((f32[128,384]{1,0:T(8,128)S(1)}, f32[128,384]{1,0:T(8,128)S(1)}, u32[]{:S(2)}, u32[]{:S(2)}) %collective-permute-start.33) | collective-permute-done | bytes 196640 | tf_op jit(solution)/shard_map/ppermute | solution.py:229
  326.4 3.7 collective-permute-done.34
  343.3 4.8 %collective-permute-done.28 = f32[128,384]{1,0:T(8,128)S(1)} collective-permute-done((f32[128,384]{1,0:T(8,128)S(1)}, f32[128,384]{1,0:T(8,128)S(1)}, u32[]{:S(2)}, u32[]{:S(2)}) %collective-permute-start.28) | collective-permute-done | bytes 196640 | tf_op jit(solution)/shard_map/ppermute | solution.py:233
  353.7 5.5 %collective-permute-done.29 = f32[256,384]{1,0:T(8,128)S(1)} collective-permute-done((f32[256,384]{1,0:T(8,128)S(1)}, f32[256,384]{1,0:T(8,128)S(1)}, u32[]{:S(2)}, u32[]{:S(2)}) %collective-permute-start.29) | collective-permute-done | bytes 393248 | tf_op jit(solution)/shard_map/ppermute | solution.py:233
  359.7 4.7 %far_gradients.1 = (bf16[256,1024]{1,0:T(8,128)(2,1)}, f32[256,128]{1,0:T(8,128)S(1)}) custom-call(bf16[256,1024]{1,0:T(8,128)(2,1)S(1)} %copy-done.9, bf16[256,128]{1,0:T(8,128)(2,1)S(1)} %copy-done.16, f32[8,256,8]{2,1,0:T(8,128)S(1)} %bitcast.341, f32[2,1024,128]{2,1,0:T(8,128)S(1)} %pad_maximum_fusion.1.exit_ref, ...), custom_call_target="tpu_custom_call" | custom-call | flops 671088640 | bytes 3538944 | tf_op jit(solution)/shard_map/far_gradients/pallas_call | solution.py:200
  367.7 3.6 collective-permute-done.30
  (659 shorter events, 200.4 us)
Async XLA Ops:
  13.4 133.1 %collective-permute-start.2 = (f32[2,256,128]{2,1,0:T(8,128)}, f32[2,256,128]{2,1,0:T(8,128)S(1)}, u32[]{:S(2)}, u32[]{:S(2)}) collective-permute-start(f32[2,256,128]{2,1,0:T(8,128)} %get-tuple-element.150), channel_id=1, source_target_pairs={{0,6},{2,4},{4,2},{6,0},{8,14},{10,12},{12,10},{14,8},{16,22},{18,... | collective-permute-start | bytes 786440 | tf_op jit(solution)/shard_map/ppermute | solution.py:253
  17.3 129.2 %collective-permute-start.1 = (f32[2,256,128]{2,1,0:T(8,128)}, f32[2,256,128]{2,1,0:T(8,128)S(1)}, u32[]{:S(2)}, u32[]{:S(2)}) collective-permute-start(f32[2,256,128]{2,1,0:T(8,128)} %get-tuple-element.151), channel_id=1, source_target_pairs={{0,4},{2,6},{4,0},{6,2},{8,12},{10,14},{12,8},{14,10},{16,20},{18,... | collective-permute-start | bytes 786440 | tf_op jit(solution)/shard_map/ppermute | solution.py:253
  17.8 128.7 %collective-permute-start = (f32[2,256,128]{2,1,0:T(8,128)S(1)}, f32[2,256,128]{2,1,0:T(8,128)S(1)}, u32[]{:S(2)}, u32[]{:S(2)}) collective-permute-start(f32[2,256,128]{2,1,0:T(8,128)S(1)} %get-tuple-element.152), channel_id=1, source_target_pairs={{0,2},{2,0},{4,6},{6,4},{8,10},{10,8},{12,14},{14,12},{16,18},{18,... | collective-permute-start | bytes 786440 | tf_op jit(solution)/shard_map/ppermute | solution.py:253
  147.7 12.6 %collective-permute-start.3 = (f32[256,128]{1,0:T(8,128)S(1)}, f32[256,128]{1,0:T(8,128)S(1)}, u32[]{:S(2)}, u32[]{:S(2)}) collective-permute-start(f32[256,128]{1,0:T(8,128)S(1)} %get-tuple-element.135), channel_id=1, source_target_pairs={{0,8},{2,10},{4,12},{6,14},{8,16},{10,18},{12,20},{14,22},{16,24},... | collective-permute-start | bytes 393224 | tf_op jit(solution)/shard_map/ppermute | solution.py:293
  175.5 10.6 %collective-permute-start.9 = (f32[2,256,128]{2,1,0:T(8,128)S(1)}, f32[2,256,128]{2,1,0:T(8,128)S(1)}, u32[]{:S(2)}, u32[]{:S(2)}) collective-permute-start(f32[2,256,128]{2,1,0:T(8,128)S(1)} %pad_maximum_fusion.9), channel_id=1, source_target_pairs={{0,6},{2,4},{4,2},{6,0},{8,14},{10,12},{12,10},{14,8},{16,22},{18,... | collective-permute-start | bytes 786440 | tf_op jit(solution)/shard_map/ppermute | solution.py:315
  190.2 18.7 %collective-permute-start.10 = (f32[256,2]{1,0:T(8,128)S(1)}, f32[256,2]{1,0:T(8,128)S(1)}, u32[]{:S(2)}, u32[]{:S(2)}) collective-permute-start(f32[256,2]{1,0:T(8,128)S(1)} %get-tuple-element.23), channel_id=1, source_target_pairs={{0,1},{1,0},{2,3},{3,2},{4,5},{5,4},{6,7},{7,6},{8,9},{9,8},{10,11... | collective-permute-start | bytes 6152 | tf_op jit(solution)/shard_map/ppermute | solution.py:218
  221.8 11.0 %collective-permute-start.13 = (f32[2,256,128]{2,1,0:T(8,128)S(1)}, f32[2,256,128]{2,1,0:T(8,128)S(1)}, u32[]{:S(2)}, u32[]{:S(2)}) collective-permute-start(f32[2,256,128]{2,1,0:T(8,128)S(1)} %get-tuple-element.145), channel_id=1, source_target_pairs={{0,6},{2,4},{4,2},{6,0},{8,14},{10,12},{12,10},{14,8},{16,22},{18,... | collective-permute-start | bytes 786440 | tf_op jit(solution)/shard_map/ppermute | solution.py:253
  222.0 14.5 %collective-permute-start.12 = (f32[2,256,128]{2,1,0:T(8,128)S(1)}, f32[2,256,128]{2,1,0:T(8,128)S(1)}, u32[]{:S(2)}, u32[]{:S(2)}) collective-permute-start(f32[2,256,128]{2,1,0:T(8,128)S(1)} %get-tuple-element.146), channel_id=1, source_target_pairs={{0,4},{2,6},{4,0},{6,2},{8,12},{10,14},{12,8},{14,10},{16,20},{18,... | collective-permute-start | bytes 786440 | tf_op jit(solution)/shard_map/ppermute | solution.py:253
  223.3 13.3 %collective-permute-start.11 = (f32[2,256,128]{2,1,0:T(8,128)S(1)}, f32[2,256,128]{2,1,0:T(8,128)S(1)}, u32[]{:S(2)}, u32[]{:S(2)}) collective-permute-start(f32[2,256,128]{2,1,0:T(8,128)S(1)} %get-tuple-element.147), channel_id=1, source_target_pairs={{0,2},{2,0},{4,6},{6,4},{8,10},{10,8},{12,14},{14,12},{16,18},{18,... | collective-permute-start | bytes 786440 | tf_op jit(solution)/shard_map/ppermute | solution.py:253
  232.3 132.1 %collective-permute-start.22 = (f32[256,128]{1,0:T(8,128)S(1)}, f32[256,128]{1,0:T(8,128)S(1)}, u32[]{:S(2)}, u32[]{:S(2)}) collective-permute-start(f32[256,128]{1,0:T(8,128)S(1)} %get-tuple-element.31), channel_id=1, source_target_pairs={{0,1},{1,0},{2,3},{3,2},{4,5},{5,4},{6,7},{7,6},{8,9},{9,8},{10,11... | collective-permute-start | bytes 393224 | tf_op jit(solution)/shard_map/ppermute | solution.py:218
  232.5 25.6 %collective-permute-start.39 = (f32[512,256]{1,0:T(8,128)S(1)}, f32[512,256]{1,0:T(8,128)S(1)}, u32[]{:S(2)}, u32[]{:S(2)}) collective-permute-start(f32[512,256]{1,0:T(8,128)S(1)} %dynamic-slice_bitcast_fusion.2), channel_id=1, source_target_pairs={{0,8},{2,10},{4,12},{6,14},{8,0},{10,2},{12,4},{14,6},{16,24},{18,... | collective-permute-start | bytes 1572872 | tf_op jit(solution)/shard_map/ppermute | solution.py:229
  232.7 64.9 %collective-permute-start.31 = (f32[512,384]{1,0:T(8,128)S(1)}, f32[512,384]{1,0:T(8,128)S(1)}, u32[]{:S(2)}, u32[]{:S(2)}) collective-permute-start(f32[512,384]{1,0:T(8,128)S(1)} %dynamic-slice_bitcast_fusion), channel_id=1, source_target_pairs={{0,4},{2,6},{4,0},{6,2},{8,12},{10,14},{12,8},{14,10},{16,20},{18,... | collective-permute-start | bytes 2359304 | tf_op jit(solution)/shard_map/ppermute | solution.py:229
  237.0 10.5 %collective-permute-start.14 = (f32[256,128]{1,0:T(8,128)S(1)}, f32[256,128]{1,0:T(8,128)S(1)}, u32[]{:S(2)}, u32[]{:S(2)}) collective-permute-start(f32[256,128]{1,0:T(8,128)S(1)} %get-tuple-element.133), channel_id=1, source_target_pairs={{0,8},{2,10},{4,12},{6,14},{8,16},{10,18},{12,20},{14,22},{16,24},... | collective-permute-start | bytes 393224 | tf_op jit(solution)/shard_map/ppermute | solution.py:293
  238.5 68.5 %collective-permute-start.23 = (f32[512,384]{1,0:T(8,128)S(1)}, f32[512,384]{1,0:T(8,128)S(1)}, u32[]{:S(2)}, u32[]{:S(2)}) collective-permute-start(f32[512,384]{1,0:T(8,128)S(1)} %dynamic-slice_bitcast_fusion.1), channel_id=1, source_target_pairs={{0,2},{2,0},{4,6},{6,4},{8,10},{10,8},{12,14},{14,12},{16,18},{18,... | collective-permute-start | bytes 2359304 | tf_op jit(solution)/shard_map/ppermute | solution.py:229
  258.1 16.1 %collective-permute-start.17 = (f32[256,128]{1,0:T(8,128)S(1)}, f32[256,128]{1,0:T(8,128)S(1)}, u32[]{:S(2)}, u32[]{:S(2)}) collective-permute-start(f32[256,128]{1,0:T(8,128)S(1)} %multiply_add_fusion.1), channel_id=1, source_target_pairs={{16,0},{18,2},{20,4},{22,6},{24,8},{26,10},{28,12},{30,14},{17,1},... | collective-permute-start | bytes 393224 | tf_op jit(solution)/shard_map/ppermute | solution.py:293
  260.5 18.6 %collective-permute-start.40 = (f32[256,256]{1,0:T(8,128)S(1)}, f32[256,256]{1,0:T(8,128)S(1)}, u32[]{:S(2)}, u32[]{:S(2)}) collective-permute-start(f32[256,256]{1,0:T(8,128)S(1)} %dynamic-slice_bitcast_fusion.5), channel_id=1, source_target_pairs={{0,16},{2,18},{4,20},{6,22},{8,24},{10,26},{12,28},{14,30},{16,0},... | collective-permute-start | bytes 786440 | tf_op jit(solution)/shard_map/ppermute | solution.py:229
  279.1 13.2 %collective-permute-start.19 = (f32[2,256,128]{2,1,0:T(8,128)S(1)}, f32[2,256,128]{2,1,0:T(8,128)S(1)}, u32[]{:S(2)}, u32[]{:S(2)}) collective-permute-start(f32[2,256,128]{2,1,0:T(8,128)S(1)} %pad_maximum_fusion.11), channel_id=1, source_target_pairs={{0,4},{2,6},{4,0},{6,2},{8,12},{10,14},{12,8},{14,10},{16,20},{18,... | collective-permute-start | bytes 786440 | tf_op jit(solution)/shard_map/ppermute | solution.py:315
  281.7 10.7 %collective-permute-start.20 = (f32[2,256,128]{2,1,0:T(8,128)S(1)}, f32[2,256,128]{2,1,0:T(8,128)S(1)}, u32[]{:S(2)}, u32[]{:S(2)}) collective-permute-start(f32[2,256,128]{2,1,0:T(8,128)S(1)} %pad_maximum_fusion.12), channel_id=1, source_target_pairs={{0,6},{2,4},{4,2},{6,0},{8,14},{10,12},{12,10},{14,8},{16,22},{18,... | collective-permute-start | bytes 786440 | tf_op jit(solution)/shard_map/ppermute | solution.py:315
  312.1 14.2 %collective-permute-start.45 = (f32[256,256]{1,0:T(8,128)S(1)}, f32[256,256]{1,0:T(8,128)S(1)}, u32[]{:S(2)}, u32[]{:S(2)}) collective-permute-start(f32[256,256]{1,0:T(8,128)S(1)} %pad_maximum_fusion.13), channel_id=1, source_target_pairs={{0,16},{2,18},{4,20},{6,22},{8,24},{10,26},{12,28},{14,30},{16,0},... | collective-permute-start | bytes 786440 | tf_op jit(solution)/shard_map/ppermute | solution.py:233
  315.1 11.1 %collective-permute-start.25 = (f32[128,384]{1,0:T(8,128)S(1)}, f32[128,384]{1,0:T(8,128)S(1)}, u32[]{:S(2)}, u32[]{:S(2)}) collective-permute-start(f32[128,384]{1,0:T(8,128)S(1)} %dynamic-slice_bitcast_fusion.13), channel_id=1, source_target_pairs={{0,8},{2,10},{4,12},{6,14},{8,0},{10,2},{12,4},{14,6},{16,24},{18,... | collective-permute-start | bytes 589832 | tf_op jit(solution)/shard_map/ppermute | solution.py:229
  348.1 11.0 %collective-permute-start.29 = (f32[256,384]{1,0:T(8,128)S(1)}, f32[256,384]{1,0:T(8,128)S(1)}, u32[]{:S(2)}, u32[]{:S(2)}) collective-permute-start(f32[256,384]{1,0:T(8,128)S(1)} %pad_maximum_fusion.5), channel_id=1, source_target_pairs={{0,4},{2,6},{4,0},{6,2},{8,12},{10,14},{12,8},{14,10},{16,20},{18,... | collective-permute-start | bytes 1179656 | tf_op jit(solution)/shard_map/ppermute | solution.py:233
  349.7 16.7 %collective-permute-start.46 = (f32[512,256]{1,0:T(8,128)S(1)}, f32[512,256]{1,0:T(8,128)S(1)}, u32[]{:S(2)}, u32[]{:S(2)}) collective-permute-start(f32[512,256]{1,0:T(8,128)S(1)} %pad_maximum_fusion.4), channel_id=1, source_target_pairs={{0,8},{2,10},{4,12},{6,14},{8,0},{10,2},{12,4},{14,6},{16,24},{18,... | collective-permute-start | bytes 1572872 | tf_op jit(solution)/shard_map/ppermute | solution.py:233
  351.0 16.6 %collective-permute-start.38 = (f32[512,384]{1,0:T(8,128)S(1)}, f32[512,384]{1,0:T(8,128)S(1)}, u32[]{:S(2)}, u32[]{:S(2)}) collective-permute-start(f32[512,384]{1,0:T(8,128)S(1)} %pad_maximum_fusion.3), channel_id=1, source_target_pairs={{0,4},{2,6},{4,0},{6,2},{8,12},{10,14},{12,8},{14,10},{16,20},{18,... | collective-permute-start | bytes 2359304 | tf_op jit(solution)/shard_map/ppermute | solution.py:233
  359.3 12.1 %collective-permute-start.30 = (f32[512,384]{1,0:T(8,128)S(1)}, f32[512,384]{1,0:T(8,128)S(1)}, u32[]{:S(2)}, u32[]{:S(2)}) collective-permute-start(f32[512,384]{1,0:T(8,128)S(1)} %pad_maximum_fusion.2), channel_id=1, source_target_pairs={{0,2},{2,0},{4,6},{6,4},{8,10},{10,8},{12,14},{14,12},{16,18},{18,... | collective-permute-start | bytes 2359304 | tf_op jit(solution)/shard_map/ppermute | solution.py:233
  (107 other events, 2450.8 us)

commit v2 on v1

v2 whole, which is shorter than its diff:
```python
import functools

import jax
import jax.numpy as jnp
from jax import lax
from jax.experimental import pallas as pl
from jax.experimental.pallas import tpu as pltpu
from jax.sharding import PartitionSpec as P

HEAD_DIM = 64
PAIR = 2 * HEAD_DIM
QUAD = 4
F32 = jnp.float32
BF16 = jnp.bfloat16
eps_norm = 1e-05
weight_scale = 0.0078125
VMEM_BYTES = 48 * 1024 * 1024


def dot(a, b, ca, cb):
    return lax.dot_general(a, b, (((ca,), (cb,)), ((), ())), preferred_element_type=F32)


def split(a):
    high = a.astype(BF16)
    return high, (a - high.astype(F32)).astype(BF16)


def dot_split_left(a, b, ca, cb):
    high, low = split(a)
    return dot(high, b, ca, cb) + dot(low, b, ca, cb)


def dot_split_right(a, b, ca, cb):
    high, low = split(b)
    return dot(a, high, ca, cb) + dot(a, low, ca, cb)


def dot_split_both(a, b, ca, cb):
    a_high, a_low = split(a)
    b_high, b_low = split(b)
    return dot(a_high, b_high, ca, cb) + (dot(a_high, b_low, ca, cb) + dot(a_low, b_high, ca, cb))


def by_head(first, second, frames):
    lane = lax.broadcasted_iota(jnp.int32, (frames, PAIR), 1)
    return jnp.where(lane < HEAD_DIM, first, second)


def pair_column(cols, at, frames):
    return by_head(cols[:, at : at + 1], cols[:, 4 + at : 5 + at], frames)


def pair_weights(cols, rows, e, frames, later_rows):
    f_col, b_col = cols[:, 4 * e : 4 * e + 1], cols[:, 4 * e + 1 : 4 * e + 2]
    f_row, b_row = rows[4 * e : 4 * e + 1, :], rows[4 * e + 1 : 4 * e + 2, :]
    i = lax.broadcasted_iota(jnp.int32, (frames, frames), 0)
    j = lax.broadcasted_iota(jnp.int32, (frames, frames), 1)
    if later_rows:
        power = jnp.where(i >= j, f_col - f_row, b_row - b_col)
    else:
        power = jnp.where(j >= i, f_row - f_col, b_col - b_row)
    weight = jnp.exp(power)
    return jnp.where(i == j, 2.0 * weight, weight)


def pick(refs):
    part = pl.program_id(0) // (pl.num_programs(0) // len(refs))
    value = refs[0][...]
    for r in range(1, len(refs)):
        value = jnp.where(part == r, refs[r][...], value)
    return value


def put(refs, up, down):
    part = pl.program_id(0) // (pl.num_programs(0) // len(refs))
    for r, ref in enumerate(refs):
        @pl.when(part == r)
        def _():
            ref[0] = up
            ref[1] = down


def state_kernel(order_ref, x_ref, b_ref, cols_ref, *out_refs):
    frames = x_ref.shape[0]
    cols = cols_ref[0]
    x = x_ref[...].astype(F32)
    tail = jnp.exp(pair_column(cols, 2, frames))
    lead = jnp.exp(pair_column(cols, 1, frames))
    put(out_refs, dot_split_left(x * tail, b_ref[...], 0, 0),
        dot_split_left(x * lead, b_ref[...], 0, 0))


def within_kernel(order_ref, x_ref, b_ref, c_ref, cols_ref, rows_ref, w_ref, d_ref, gain_ref, skip_ref,
                  y_ref, m_ref, scores):
    frames = x_ref.shape[0]

    @pl.when(pl.program_id(0) == 0)
    def _():
        scores[...] = dot(c_ref[...], b_ref[...], 1, 1)

    cols, rows = cols_ref[0], rows_ref[0]
    x = x_ref[...]
    parts = []
    for e in range(2):
        pw = pair_weights(cols, rows, e, frames, True) * scores[...]
        parts.append(dot_split_left(pw, x, 1, 0))
    y_ref[...] = by_head(parts[0], parts[1], frames) + skip_ref[...] * x.astype(F32)
    m_ref[...] = dot(d_ref[...], w_ref[...], 1, 1) * gain_ref[...]


def merge_kernel(quad, order_ref, near_ref, m_ref, z_ref, c_ref, cols_ref, *refs):
    entry = pick(refs[:quad])
    y_ref, sums_ref, sq, cross = refs[quad:]
    frames = near_ref.shape[0]
    step = pl.program_id(0)

    @pl.when(step == 0)
    def _():
        sq[...] = jnp.zeros_like(sq)
        cross[...] = jnp.zeros_like(cross)

    cols = cols_ref[0]
    c = c_ref[...]
    y = near_ref[...]
    y = y + jnp.exp(pair_column(cols, 0, frames)) * dot_split_right(c, entry[0], 1, 1)
    y = y + jnp.exp(pair_column(cols, 3, frames)) * dot_split_right(c, entry[1], 1, 1)
    y_ref[...] = y
    z = z_ref[...].astype(F32)
    u = y * z * (1.0 / (1.0 + jnp.exp(-z)))
    sq[...] += u * u
    cross[...] += u * m_ref[...]

    @pl.when(step == pl.num_programs(0) - 1)
    def _():
        sums_ref[:, 0:1] = jnp.sum(sq[...], axis=1, keepdims=True)
        sums_ref[:, 1:2] = jnp.sum(cross[...], axis=1, keepdims=True)


def turn_kernel(inner, quad, order_ref, y_ref, m_ref, z_ref, c_ref, cols_ref, sums_ref, gain_ref,
                d_ref, dy_ref, gz_ref, *refs):
    back_refs, w_refs = refs[:quad], refs[quad:]
    frames = y_ref.shape[0]
    cols = cols_ref[0]
    y = y_ref[...]
    z = z_ref[...].astype(F32)
    sig = 1.0 / (1.0 + jnp.exp(-z))
    silu = z * sig
    u = y * silu
    q = lax.rsqrt(sums_ref[:, 0:1] * (1.0 / inner) + eps_norm)
    k = sums_ref[:, 1:2] * (1.0 / inner)
    du = q * m_ref[...] - u * (q * q * q * k)
    dy = du * silu
    dy_ref[...] = dy
    gz_ref[...] = (du * y * sig * (1.0 + z * (1.0 - sig))).astype(BF16)
    n = (u * q * gain_ref[...]).astype(BF16)
    c = c_ref[...]
    put(back_refs, dot_split_left(dy * jnp.exp(pair_column(cols, 3, frames)), c, 0, 0),
        dot_split_left(dy * jnp.exp(pair_column(cols, 0, frames)), c, 0, 0))
    at = 0
    for w_ref in w_refs:
        columns = w_ref.shape[1]
        w_ref[...] = dot(n, d_ref[:, at : at + columns], 0, 0) * weight_scale
        at += columns


def near_kernel(quad, order_ref, x_ref, b_ref, c_ref, cols_ref, rows_ref, skip_ref, dy_ref, *refs):
    entry = pick(refs[:quad])
    gx_ref, gb_ref, gc_ref, scores, pairs = refs[quad:]
    frames = x_ref.shape[0]
    step = pl.program_id(0)

    @pl.when(step == 0)
    def _():
        scores[...] = dot(b_ref[...], c_ref[...], 1, 1)
        pairs[...] = jnp.zeros_like(pairs)
        gc_ref[...] = jnp.zeros_like(gc_ref)

    cols, rows = cols_ref[0], rows_ref[0]
    x = x_ref[...]
    dy = dy_ref[...]
    lane = lax.broadcasted_iota(jnp.int32, (frames, PAIR), 1)
    parts = []
    for e in range(2):
        weight = pair_weights(cols, rows, e, frames, False)
        own = (lane < HEAD_DIM) if e == 0 else (lane >= HEAD_DIM)
        dy_own = jnp.where(own, dy, 0.0)
        pairs[...] += weight * dot_split_right(x, dy_own, 1, 1)
        parts.append(dot_split_both(weight * scores[...], dy_own, 1, 0))
    gx_ref[...] = parts[0] + parts[1] + skip_ref[...] * dy
    gc_ref[...] += dot_split_both(dy * jnp.exp(pair_column(cols, 0, frames)), entry[0], 1, 0)
    gc_ref[...] += dot_split_both(dy * jnp.exp(pair_column(cols, 3, frames)), entry[1], 1, 0)

    @pl.when(step == pl.num_programs(0) - 1)
    def _():
        gb_ref[...] = dot_split_left(pairs[...], c_ref[...], 1, 0)
        gc_ref[...] += dot_split_left(pairs[...], b_ref[...], 0, 0)


def far_kernel(quad, order_ref, x_ref, b_ref, cols_ref, near_ref, gb_near_ref, *refs):
    leave = pick(refs[:quad])
    gx_ref, gb_ref = refs[quad:]
    frames = x_ref.shape[0]

    @pl.when(pl.program_id(0) == 0)
    def _():
        gb_ref[...] = gb_near_ref[...]

    cols = cols_ref[0]
    b = b_ref[...]
    x = x_ref[...].astype(F32)
    tail = jnp.exp(pair_column(cols, 2, frames))
    lead = jnp.exp(pair_column(cols, 1, frames))
    far = tail * dot_split_right(b, leave[1], 1, 1) + lead * dot_split_right(b, leave[0], 1, 1)
    gx_ref[...] = (near_ref[...] + far).astype(BF16)
    gb_ref[...] += dot_split_both(x * tail, leave[1], 1, 0)
    gb_ref[...] += dot_split_both(x * lead, leave[0], 1, 0)


def call(kernel, name, order, ins, in_specs, outs, out_specs, scratch=(), flops=0):
    moved = sum(a.size * a.dtype.itemsize for a in ins) + sum(
        o.size * o.dtype.itemsize for o in outs)
    return pl.pallas_call(
        kernel,
        name=name,
        grid_spec=pltpu.PrefetchScalarGridSpec(
            num_scalar_prefetch=1,
            grid=(order.shape[0],),
            in_specs=in_specs,
            out_specs=out_specs,
            scratch_shapes=list(scratch),
        ),
        out_shape=outs,
        compiler_params=pltpu.CompilerParams(
            dimension_semantics=("arbitrary",), vmem_limit_bytes=VMEM_BYTES),
        cost_estimate=pl.CostEstimate(flops=flops, bytes_accessed=moved, transcendentals=0),
    )(order, *ins)


def small_call(kernel, name, factors, ins, outs):
    moved = sum(a.size * 4 for a in ins) + sum(o.size * 4 for o in outs)
    vmem = pl.BlockSpec(memory_space=pltpu.VMEM)
    return pl.pallas_call(
        kernel,
        name=name,
        in_specs=[pl.BlockSpec(memory_space=pltpu.SMEM)] + [vmem] * len(ins),
        out_specs=[vmem] * len(outs),
        out_shape=outs,
        compiler_params=pltpu.CompilerParams(vmem_limit_bytes=VMEM_BYTES),
        cost_estimate=pl.CostEstimate(flops=0, bytes_accessed=moved, transcendentals=0),
    )(factors, *ins)


def sum_over(value, axis):
    size = lax.axis_size(axis)
    reach = 1
    while reach < size:
        value = value + lax.ppermute(value, axis, [(i, i ^ reach) for i in range(size)])
        reach *= 2
    return value


def sum_slabs(value, bits):
    size, me = lax.axis_size("seq"), lax.axis_index("seq")
    for bit in bits:
        mine = (me >> bit) & 1
        halves = value.reshape(2, value.shape[0] // 2, value.shape[1])
        sent = lax.dynamic_index_in_dim(halves, 1 - mine, 0, keepdims=False)
        came = lax.ppermute(sent, "seq", [(i, i ^ (1 << bit)) for i in range(size)])
        value = lax.dynamic_index_in_dim(halves, mine, 0, keepdims=False) + came
    for bit in reversed(bits):
        mine = (me >> bit) & 1
        came = lax.ppermute(value, "seq", [(i, i ^ (1 << bit)) for i in range(size)])
        first = jnp.where(mine == 0, value, came)
        second = jnp.where(mine == 0, came, value)
        value = jnp.concatenate([first, second], axis=0)
    return value


def factor_reader(factors_ref, quad, heads, steps):
    kinds = 1 + 2 * quad + quad * quad + steps

    def read(d, kind, h):
        return factors_ref[(d * kinds + kind) * heads + h]

    return read


def total_kernel(quad, heads, steps, factors_ref, *refs):
    read = factor_reader(factors_ref, quad, heads, steps)
    for d in range(2):
        for h in range(heads):
            at = slice(h * HEAD_DIM, (h + 1) * HEAD_DIM)
            total = read(d, 0, h) * refs[0][d, at, :]
            for r in range(1, quad):
                total = total + read(d, r, h) * refs[r][d, at, :]
            refs[quad + d][at, :] = total


def advance_kernel(quad, heads, steps, k, factors_ref, *refs):
    read = factor_reader(factors_ref, quad, heads, steps)
    totals, came, before, sent, after = refs[:2], refs[2:4], refs[4:-4], refs[-4:-2], refs[-2:]
    for d in range(2):
        for h in range(heads):
            at = slice(h * HEAD_DIM, (h + 1) * HEAD_DIM)
            entering = came[d][at, :]
            if k:
                passed = read(d, 1 + 2 * quad + quad * quad + k, h)
                entering = before[d][at, :] + passed * entering
            after[d][at, :] = entering
            sent[d][at, :] = totals[d][at, :] + read(d, quad, h) * entering


def reply_kernel(quad, heads, steps, factors_ref, *refs):
    read = factor_reader(factors_ref, quad, heads, steps)
    held, came, before, replies = refs[:quad], refs[quad : quad + 2], refs[quad + 2 : -quad], refs[-quad:]
    k = steps - 1
    for d in range(2):
        for h in range(heads):
            at = slice(h * HEAD_DIM, (h + 1) * HEAD_DIM)
            entering = came[d][at, :]
            if k:
                passed = read(d, 1 + 2 * quad + quad * quad + k, h)
                entering = before[d][at, :] + passed * entering
            states = [held[s][d, at, :] for s in range(quad)]
            for r in range(quad):
                reply = read(d, quad + 1 + r, h) * entering
                for s in range(quad):
                    if s != r:
                        reply = reply + read(d, 1 + 2 * quad + s * quad + r, h) * states[s]
                replies[r][d, at, :] = reply


def scan_factors(ends_f, ends_b, quad, steps):
    size, me = lax.axis_size("seq"), lax.axis_index("seq")
    heads = ends_f.shape[0]
    table = jnp.concatenate([ends_f, ends_b])[None, :]
    reach = 1
    while reach < size:
        came = lax.ppermute(table, "seq", [(i, i ^ reach) for i in range(size)])
        table = jnp.concatenate([table, came], axis=0)
        reach *= 2
    none = -1
    runs = [(r, 0, none, quad) for r in range(quad)]
    runs += [(none, -1, none, quad)]
    runs += [(none, -1, r, 0) for r in range(quad)]
    runs += [(s, 0, r, 0) for s in range(quad) for r in range(quad)]
    runs += [(none, -(2 ** k - 1) * quad - 1, none, 0) for k in range(steps)]
    low_xor, low_add, high_xor, high_add = (jnp.array(v, jnp.int32) for v in zip(*runs))
    place = jnp.stack([me, size - 1 - me])[:, None]
    base = place // quad * quad
    low = jnp.where(low_xor == none, base + low_add, place ^ low_xor)
    high = jnp.where(high_xor == none, base + high_add, place ^ high_xor)
    slab = (place ^ jnp.arange(size, dtype=jnp.int32))[:, None, :]
    inside = (slab > low[:, :, None]) & (slab < high[:, :, None])
    logs = table.reshape(1, 1, size, 2 * heads)
    powers = jnp.sum(jnp.where(inside[..., None], logs, 0.0), axis=2)
    factors = jnp.where((low < high)[..., None], jnp.exp(powers), 0.0)
    return factors.reshape(2, len(runs), 2, heads)


def carry(mine, factors, quad, steps):
    size = lax.axis_size("seq")
    _, rows, width = mine[0].shape
    heads = rows // HEAD_DIM
    both = jax.ShapeDtypeStruct((2, rows, width), F32)
    one = jax.ShapeDtypeStruct((rows, width), F32)
    sizes = (quad, heads, steps)

    def trade(parts):
        return [parts[0]] + [
            lax.ppermute(parts[r], "seq", [(i, i ^ r) for i in range(size)])
            for r in range(1, quad)]

    held = trade(mine)
    totals = small_call(
        functools.partial(total_kernel, *sizes), "group_totals", factors, held, [one, one])
    sent, before = totals, []
    for k in range(steps):
        came = []
        for d, sign in enumerate((1, -1)):
            shift = sign * quad * 2 ** k
            came.append(lax.ppermute(
                sent[d], "seq", [(i, i + shift) for i in range(size) if 0 <= i + shift < size]))
        if k < steps - 1:
            new = small_call(
                functools.partial(advance_kernel, *sizes, k), "advance_scan", factors,
                [*totals, *came, *before], [one] * 4)
            sent, before = new[:2], new[2:]
    replies = small_call(
        functools.partial(reply_kernel, *sizes), "group_replies", factors,
        [*held, *came, *before], [both] * quad)
    return trade(replies)


def body(x_in, gate_in, b_in, c_in, decay_fwd, decay_bwd, skip_gain, norm_gain, w_out, d_out):
    frames, width = x_in.shape
    heads = decay_fwd.shape[0]
    state = b_in.shape[1]
    model = d_out.shape[1]
    pairs = heads // 2
    inner = width * lax.axis_size("head")

    fwd = jnp.cumsum(decay_fwd, axis=1)
    bwd = jnp.cumsum(decay_bwd, axis=1) - decay_bwd
    fwd_end = fwd[:, -1:]
    bwd_end = bwd[:, -1:] + decay_bwd[:, -1:]
    lines = jnp.stack([fwd, bwd, fwd_end - fwd, bwd_end - bwd], axis=1)
    rows = lines.reshape(pairs, 8, frames)
    cols = rows.transpose(0, 2, 1)
    quad = min(QUAD, pairs)
    per_part = pairs // quad
    part_heads = heads // quad
    slabs = lax.axis_size("seq")
    steps = (slabs // quad - 1).bit_length()
    q = lax.axis_index("seq") % quad
    turn = jnp.arange(pairs, dtype=jnp.int32)
    order = ((turn // per_part) ^ q) * per_part + turn % per_part
    factors = scan_factors(fwd_end[:, 0], bwd_end[:, 0], quad, steps)
    factors = lax.dynamic_slice_in_dim(factors, q * part_heads, part_heads, 3)
    entry_factors = jnp.stack([factors[0, :, 0], factors[1, :, 1]]).reshape(-1)
    exit_factors = jnp.stack([factors[0, :, 1], factors[1, :, 0]]).reshape(-1)
    skip = jnp.repeat(skip_gain, HEAD_DIM)[None, :]
    gain = norm_gain[None, :]

    wide = pl.BlockSpec((frames, PAIR), lambda i, p: (0, p[i]))
    narrow = pl.BlockSpec((frames, state), lambda i, p: (0, 0))
    col = pl.BlockSpec((1, frames, 8), lambda i, p: (p[i], 0, 0))
    row = pl.BlockSpec((1, 8, frames), lambda i, p: (p[i], 0, 0))
    lanes = pl.BlockSpec((1, PAIR), lambda i, p: (0, p[i]))
    states = [
        pl.BlockSpec((2, PAIR, state),
                     lambda i, p, r=r: (0, jnp.clip(i - r * per_part, 0, per_part - 1), 0))
        for r in range(quad)]
    model_rows = pl.BlockSpec((frames, model), lambda i, p: (0, 0))
    weight_rows = pl.BlockSpec((PAIR, model), lambda i, p: (p[i], 0))
    sums_spec = pl.BlockSpec((frames, 2), lambda i, p: (0, 0))
    shape = jax.ShapeDtypeStruct
    wide_f32, wide_bf16 = shape((frames, width), F32), shape((frames, width), BF16)
    state_out = [shape((2, width // quad, state), F32)] * quad
    narrow_out = shape((frames, state), F32)
    square = pltpu.VMEM((frames, frames), F32)
    lane_sums = pltpu.VMEM((frames, PAIR), F32)
    quad_flops = 2 * frames * frames * width

    local = call(state_kernel, "local_states", order, (x_in, b_in, cols), [wide, narrow, col],
                 state_out, states, flops=8 * frames * width * state)
    entry = carry(local, entry_factors, quad, steps)
    near_y, scaled = call(
        within_kernel, "within_slab", order,
        (x_in, b_in, c_in, cols, rows, w_out, d_out, gain, skip),
        [wide, narrow, narrow, col, row, weight_rows, model_rows, lanes, lanes],
        [wide_f32, wide_f32], [wide, wide], [square],
        flops=8 * quad_flops + 2 * frames * width * model)
    y, sums = call(
        functools.partial(merge_kernel, quad), "merge_entry", order,
        (near_y, scaled, gate_in, c_in, cols, *entry),
        [wide, wide, wide, narrow, col, *states],
        [wide_f32, shape((frames, 2), F32)], [wide, sums_spec], [lane_sums, lane_sums],
        flops=8 * frames * width * state)
    sums = sum_over(sums, "head")
    bits = list(range((lax.axis_size("seq") - 1).bit_length()))
    orders = (bits, [bits[1], bits[0]] + bits[2:], bits[2:] + bits[:2])
    thirds = model // 8 * 3
    chunks = (thirds, thirds, model - 2 * thirds)
    dy, grad_z, *rest = call(
        functools.partial(turn_kernel, inner, quad), "norm_backward", order,
        (y, scaled, gate_in, c_in, cols, sums, gain, d_out),
        [wide, wide, wide, narrow, col, sums_spec, lanes, model_rows],
        [wide_f32, wide_bf16, *state_out] + [shape((width, n), F32) for n in chunks],
        [wide, wide, *states] + [pl.BlockSpec((PAIR, n), lambda i, p: (p[i], 0)) for n in chunks],
        flops=2 * frames * width * model + 8 * frames * width * state)
    back, local_w = rest[:quad], rest[quad:]
    exits = carry(back, exit_factors, quad, steps)
    grad_w = jnp.concatenate(
        [sum_slabs(part, order) for part, order in zip(local_w, orders)], axis=1)
    near_x, near_b, grad_c = call(
        functools.partial(near_kernel, quad), "near_gradients", order,
        (x_in, b_in, c_in, cols, rows, skip, dy, *entry),
        [wide, narrow, narrow, col, row, lanes, wide, *states],
        [wide_f32, narrow_out, narrow_out], [wide, narrow, narrow], [square, square],
        flops=20 * quad_flops)
    grad_c = sum_over(grad_c, "head")
    grad_x, grad_b = call(
        functools.partial(far_kernel, quad), "far_gradients", order,
        (x_in, b_in, cols, near_x, near_b, *exits),
        [wide, narrow, col, wide, narrow, *states],
        [wide_bf16, narrow_out], [wide, narrow], flops=20 * frames * width * state)
    grad_b = sum_over(grad_b, "head")
    return grad_x, grad_z, grad_b, grad_c, grad_w


def solution(mesh):
    in_specs = (
        P("seq", "head"),
        P("seq", "head"),
        P("seq", None),
        P("seq", None),
        P("head", "seq"),
        P("head", "seq"),
        P("head"),
        P("head"),
        P("head", None),
        P("seq", None),
    )
    out_specs = (
        P("seq", "head"),
        P("seq", "head"),
        P("seq", None),
        P("seq", None),
        P("head", None),
    )
    return jax.shard_map(body, mesh=mesh, in_specs=in_specs, out_specs=out_specs, check_vma=False)
```

time: 376 us -> 285 us (0.76)
  local copies, waits for them, and re-layouts: 109 us -> 21.3 us
  blocking collectives: 41.4 us -> 0 us
  starting transfers between devices: 40.9 us -> 71.3 us
  Pallas kernels: 35.5 us -> 53.8 us
  other arithmetic: 24.1 us -> 14.2 us
    mul x172 -> x0, local copies, waits for them, and re-layouts: 63.3 us -> none  [scale(): return (factor * state.reshape(part_heads, -1, width)).reshape(part, width)]
    all_gather x1 -> x0, blocking collectives: 41.4 us -> none  [body(): ends = lax.all_gather(jnp.stack([fwd_end[:, 0], bwd_end[:, 0]]), 'seq')]
    exp x86 -> x2, local copies, waits for them, and re-layouts: 32 us -> 0.1 us  [scan_factors(): factors = jnp.where((low < high)[..., None], jnp.exp(powers), 0.0)]
    ppermute x20 -> x24, waiting for transfers between devices: 58.2 us -> 32.2 us  [the longest x8 26.9 us: carry(): lax.ppermute(sent[d], 'seq', [(i, i + shift) for i in range(size) if 0 <=...]
    ppermute x20 -> x24, starting transfers between devices: 24.3 us -> 47 us  [the longest x12 20.1 us: trade(): lax.ppermute(parts[r], 'seq', [(i, i ^ r) for i in range(size)])]
    pallas_call x6 -> x12, Pallas kernels: 35.5 us -> 53.8 us  [the longest x6 49 us: call(): pl.pallas_call(kernel, name=name, grid_spec=pltpu.PrefetchScalarGridSpec(...]
    ppermute x12, waiting for transfers between devices: 30.8 us -> 44.8 us  [sum_slabs(): came = lax.ppermute(sent, 'seq', [(i, i ^ 1 << bit) for i in range(size)])]
    ppermute x12, waiting for transfers between devices: 30.5 us -> 42.7 us  [sum_slabs(): came = lax.ppermute(value, 'seq', [(i, i ^ 1 << bit) for i in range(size)])]
  transfers between devices with their start and end apart: 47 -> 51, of which waited for: 30 -> 26; matrix products, arithmetic and copies ran while one was open for 30% -> 4% of each run, Pallas kernels for 5% -> 11%
where the time goes in v2:
time: 285 us; the launch traced here: 284 us
  waiting for transfers between devices  122 us (43%)
  starting transfers between devices  71.3 us (25%)
  Pallas kernels  53.8 us (19%)
  local copies, waits for them, and re-layouts  21.3 us (7%)
  other arithmetic  14.2 us (5%)
    pallas_call x6, Pallas kernels, call(): pl.pallas_call(kernel, name=name, grid_spec=pltpu.PrefetchScalarGridSpec(...  49 us
    ppermute x12, waiting for transfers between devices, sum_slabs(): came = lax.ppermute(sent, 'seq', [(i, i ^ 1 << bit) for i in range(size)])  44.8 us
    ppermute x12, waiting for transfers between devices, sum_slabs(): came = lax.ppermute(value, 'seq', [(i, i ^ 1 << bit) for i in range(size)])  42.7 us
    ppermute x8, waiting for transfers between devices, carry(): lax.ppermute(sent[d], 'seq', [(i, i + shift) for i in range(size) if 0 <=...  26.9 us
    ppermute x12, starting transfers between devices, trade(): lax.ppermute(parts[r], 'seq', [(i, i ^ r) for i in range(size)])  20.1 us
    ppermute x8, starting transfers between devices, carry(): lax.ppermute(sent[d], 'seq', [(i, i + shift) for i in range(size) if 0 <=...  17.8 us
    unnamed x70, local copies, waits for them, and re-layouts  15 us
    ppermute x12, starting transfers between devices, sum_slabs(): came = lax.ppermute(value, 'seq', [(i, i ^ 1 << bit) for i in range(size)])  12.1 us
  transfers between devices with their start and end apart: 51, of which 26 were waited for; matrix products, arithmetic and copies ran while one was open for 4% of the time, Pallas kernels for 11%

profile of v2, /device:TPU:0, one launch (start us, length us, event | category | flops | bytes accessed | tf_op | source)
XLA Modules:
  0.0 283.7 jit_solution(8739931498151901304)
XLA Ops:
  11.0 5.8 %local_states.1 = (f32[2,256,128]{2,1,0:T(8,128)S(1)}, f32[2,256,128]{2,1,0:T(8,128)}, f32[2,256,128]{2,1,0:T(8,128)S(1)}, f32[2,256,128]{2,1,0:T(8,128)S(1)}) custom-call(s32[8]{0:T(128)S(1)} %fusion.1.order_ref, bf16[256,1024]{1,0:T(8,128)(2,1)S(1)} %copy-done.4, bf16[256,128]{1,0:T(8,128)(2,1)S(1)} %copy-done.13, f32[8,256,8]{2,1,0:T(8,128)S(1)} %bitcast.98), custom_call_target="tpu_custom_call" | custom-call | flops 268435456 | bytes 1703936 | tf_op jit(solution)/shard_map/local_states/pallas_call | solution.py:223
  35.4 3.8 %collective-permute-start.7 = (f32[256,128]{1,0:T(8,128)S(1)}, f32[256,128]{1,0:T(8,128)S(1)}, u32[]{:S(2)}, u32[]{:S(2)}) collective-permute-start(f32[256,128]{1,0:T(8,128)S(1)} %get-tuple-element.53.refs_0_), channel_id=1, source_target_pairs={{0,8},{2,10},{4,12},{6,14},{8,16},{10,18},{12,20},{14,22},{16,24},... | collective-permute-start | bytes 393224 | tf_op jit(solution)/shard_map/ppermute | solution.py:383
  41.7 4.4 %collective-permute-done.8.refs_3_ = f32[256,128]{1,0:T(8,128)S(1)} collective-permute-done((f32[256,128]{1,0:T(8,128)S(1)}, f32[256,128]{1,0:T(8,128)S(1)}, u32[]{:S(2)}, u32[]{:S(2)}) %collective-permute-start.8) | collective-permute-done | bytes 131104 | tf_op jit(solution)/shard_map/ppermute | solution.py:383
  46.6 4.5 %collective-permute-start.9 = (f32[256,128]{1,0:T(8,128)S(1)}, f32[256,128]{1,0:T(8,128)S(1)}, u32[]{:S(2)}, u32[]{:S(2)}) collective-permute-start(f32[256,128]{1,0:T(8,128)S(1)} %get-tuple-element.55), channel_id=1, source_target_pairs={{0,16},{2,18},{4,20},{6,22},{8,24},{10,26},{12,28},{14,30},{1,17},... | collective-permute-start | bytes 393224 | tf_op jit(solution)/shard_map/ppermute | solution.py:383
  53.7 5.7 %collective-permute-done.10.refs_5_ = f32[256,128]{1,0:T(8,128)S(1)} collective-permute-done((f32[256,128]{1,0:T(8,128)S(1)}, f32[256,128]{1,0:T(8,128)S(1)}, u32[]{:S(2)}, u32[]{:S(2)}) %collective-permute-start.10) | collective-permute-done | bytes 131104 | tf_op jit(solution)/shard_map/ppermute | solution.py:383
  61.6 6.6 %collective-permute-start.11 = (f32[2,256,128]{2,1,0:T(8,128)}, f32[2,256,128]{2,1,0:T(8,128)}, u32[]{:S(2)}, u32[]{:S(2)}) collective-permute-start(f32[2,256,128]{2,1,0:T(8,128)} %get-tuple-element.60), channel_id=1, source_target_pairs={{0,2},{2,0},{4,6},{6,4},{8,10},{10,8},{12,14},{14,12},{16,18},{18,... | collective-permute-start | bytes 786440 | tf_op jit(solution)/shard_map/ppermute | solution.py:372
  76.4 8.1 %within_slab.1 = (f32[256,1024]{1,0:T(8,128)S(1)}, f32[256,1024]{1,0:T(8,128)S(1)}) custom-call(s32[8]{0:T(128)S(1)} %copy-done.21, bf16[256,1024]{1,0:T(8,128)(2,1)S(1)} %copy-done.5, bf16[256,128]{1,0:T(8,128)(2,1)S(1)} %copy-done.14, bf16[256,128]{1,0:T(8,128)(2,1)S(1)} %copy-done.12, f32[8,256,8]{2,1,0:T(8,128)S(1)} %bitcast.99, ...), custom_call_target="tpu_custom_call" | custom-call | flops 1610612736 | bytes 5513216 | tf_op jit(solution)/shard_map/within_slab/pallas_call | solution.py:223
  85.3 7.4 %merge_entry.1 = (f32[256,1024]{1,0:T(8,128)S(1)}, f32[256,2]{1,0:T(8,128)}) custom-call(s32[8]{0:T(128)S(1)} %copy-done.22, f32[256,1024]{1,0:T(8,128)S(1)} %get-tuple-element.47.near_ref, f32[256,1024]{1,0:T(8,128)S(1)} %get-tuple-element.48.m_ref, bf16[256,1024]{1,0:T(8,128)(2,1)S(1)} %copy-done.6, bf16[256,128]{1,0:T(8,128)(2,1)S(1)} %copy-done.12, ...), custom_call_target="tpu_custom_call" | custom-call | flops 268435456 | bytes 4851712 | tf_op jit(solution)/shard_map/merge_entry/pallas_call | solution.py:223
  99.7 12.7 %norm_backward.1 = (f32[256,1024]{1,0:T(8,128)S(1)}, bf16[256,1024]{1,0:T(8,128)(2,1)}, f32[2,256,128]{2,1,0:T(8,128)S(1)}, f32[2,256,128]{2,1,0:T(8,128)}, f32[...) custom-call(s32[8]{0:T(128)S(1)} %copy-done.23, ...), custom_call_target="tpu_custom_call" | custom-call | flops 805306368 | bytes 10098688 | tf_op jit(solution)/shard_map/norm_backward/pallas_call | solution.py:223
  118.6 10.5 %collective-permute-done.43 = f32[512,256]{1,0:T(8,128)S(1)} collective-permute-done((f32[512,256]{1,0:T(8,128)S(1)}, f32[512,256]{1,0:T(8,128)S(1)}, u32[]{:S(2)}, u32[]{:S(2)}) %collective-permute-start.43) | collective-permute-done | bytes 524320 | tf_op jit(solution)/shard_map/ppermute | solution.py:269
  139.3 8.5 %collective-permute-done.19.refs_3_ = f32[256,128]{1,0:T(8,128)S(1)} collective-permute-done((f32[256,128]{1,0:T(8,128)S(1)}, f32[256,128]{1,0:T(8,128)S(1)}, u32[]{:S(2)}, u32[]{:S(2)}) %collective-permute-start.19) | collective-permute-done | bytes 131104 | tf_op jit(solution)/shard_map/ppermute | solution.py:383
  154.8 6.0 %collective-permute-done.21.refs_5_ = f32[256,128]{1,0:T(8,128)S(1)} collective-permute-done((f32[256,128]{1,0:T(8,128)S(1)}, f32[256,128]{1,0:T(8,128)S(1)}, u32[]{:S(2)}, u32[]{:S(2)}) %collective-permute-start.21) | collective-permute-done | bytes 131104 | tf_op jit(solution)/shard_map/ppermute | solution.py:383
  166.9 5.7 %collective-permute-done.46 = f32[64,256]{1,0:T(8,128)S(1)} collective-permute-done((f32[64,256]{1,0:T(8,128)S(1)}, f32[64,256]{1,0:T(8,128)S(1)}, u32[]{:S(2)}, u32[]{:S(2)}) %collective-permute-start.46) | collective-permute-done | bytes 65568 | tf_op jit(solution)/shard_map/ppermute | solution.py:269
  179.3 17.8 %collective-permute-done.48 = f32[128,256]{1,0:T(8,128)S(1)} collective-permute-done((f32[128,256]{1,0:T(8,128)S(1)}, f32[128,256]{1,0:T(8,128)S(1)}, u32[]{:S(2)}, u32[]{:S(2)}) %collective-permute-start.48) | collective-permute-done | bytes 131104 | tf_op jit(solution)/shard_map/ppermute | solution.py:273
  202.3 4.8 %collective-permute-done.28 = f32[256,384]{1,0:T(8,128)S(1)} collective-permute-done((f32[256,384]{1,0:T(8,128)S(1)}, f32[256,384]{1,0:T(8,128)S(1)}, u32[]{:S(2)}, u32[]{:S(2)}) %collective-permute-start.28) | collective-permute-done | bytes 393248 | tf_op jit(solution)/shard_map/ppermute | solution.py:269
  208.2 8.9 %collective-permute-done.37 = f32[128,384]{1,0:T(8,128)S(1)} collective-permute-done((f32[128,384]{1,0:T(8,128)S(1)}, f32[128,384]{1,0:T(8,128)S(1)}, u32[]{:S(2)}, u32[]{:S(2)}) %collective-permute-start.37) | collective-permute-done | bytes 196640 | tf_op jit(solution)/shard_map/ppermute | solution.py:269
  217.2 6.8 %collective-permute-done.29 = f32[128,384]{1,0:T(8,128)S(1)} collective-permute-done((f32[128,384]{1,0:T(8,128)S(1)}, f32[128,384]{1,0:T(8,128)S(1)}, u32[]{:S(2)}, u32[]{:S(2)}) %collective-permute-start.29) | collective-permute-done | bytes 196640 | tf_op jit(solution)/shard_map/ppermute | solution.py:269
  227.0 6.7 %collective-permute-done.38 = f32[64,384]{1,0:T(8,128)S(1)} collective-permute-done((f32[64,384]{1,0:T(8,128)S(1)}, f32[64,384]{1,0:T(8,128)S(1)}, u32[]{:S(2)}, u32[]{:S(2)}) %collective-permute-start.38) | collective-permute-done | bytes 98336 | tf_op jit(solution)/shard_map/ppermute | solution.py:269
  236.8 6.3 %collective-permute-done.39 = f32[64,384]{1,0:T(8,128)S(1)} collective-permute-done((f32[64,384]{1,0:T(8,128)S(1)}, f32[64,384]{1,0:T(8,128)S(1)}, u32[]{:S(2)}, u32[]{:S(2)}) %collective-permute-start.39) | collective-permute-done | bytes 98336 | tf_op jit(solution)/shard_map/ppermute | solution.py:273
  245.4 5.1 %collective-permute-done.40 = f32[128,384]{1,0:T(8,128)S(1)} collective-permute-done((f32[128,384]{1,0:T(8,128)S(1)}, f32[128,384]{1,0:T(8,128)S(1)}, u32[]{:S(2)}, u32[]{:S(2)}) %collective-permute-start.40) | collective-permute-done | bytes 196640 | tf_op jit(solution)/shard_map/ppermute | solution.py:273
  253.0 5.3 %collective-permute-done.41 = f32[256,384]{1,0:T(8,128)S(1)} collective-permute-done((f32[256,384]{1,0:T(8,128)S(1)}, f32[256,384]{1,0:T(8,128)S(1)}, u32[]{:S(2)}, u32[]{:S(2)}) %collective-permute-start.41) | collective-permute-done | bytes 393248 | tf_op jit(solution)/shard_map/ppermute | solution.py:273
  258.7 3.3 %collective-permute-done.33 = f32[256,384]{1,0:T(8,128)S(1)} collective-permute-done((f32[256,384]{1,0:T(8,128)S(1)}, f32[256,384]{1,0:T(8,128)S(1)}, u32[]{:S(2)}, u32[]{:S(2)}) %collective-permute-start.33) | collective-permute-done | bytes 393248 | tf_op jit(solution)/shard_map/ppermute | solution.py:273
  263.4 9.2 %near_gradients.1 = (f32[256,1024]{1,0:T(8,128)S(1)}, f32[256,128]{1,0:T(8,128)S(1)}, f32[256,128]{1,0:T(8,128)S(1)}) custom-call(s32[8]{0:T(128)S(1)} %copy-done.24, bf16[256,1024]{1,0:T(8,128)(2,1)S(1)} %copy-done.5, bf16[256,128]{1,0:T(8,128)(2,1)S(1)} %copy-done.14, bf16[256,128]{1,0:T(8,128)(2,1)S(1)} %copy-done.12, f32[8,256,8]{2,1,0:T(8,128)S(1)} %bitcast.102, ...), custom_call_target="tpu_custom_call" | custom-call | flops 2684354560 | bytes 4198400 | tf_op jit(solution)/shard_map/near_gradients/pallas_call | solution.py:223
  272.7 5.9 %far_gradients.1 = (bf16[256,1024]{1,0:T(8,128)(2,1)}, f32[256,128]{1,0:T(8,128)S(1)}) custom-call(s32[8]{0:T(128)S(1)} %copy-done.24, bf16[256,1024]{1,0:T(8,128)(2,1)S(1)} %copy-done.5, bf16[256,128]{1,0:T(8,128)(2,1)S(1)} %copy-done.14, f32[8,256,8]{2,1,0:T(8,128)S(1)} %bitcast.103, f32[256,1024]{1,0:T(8,128)S(1)} %get-tuple-element.66.near_ref, ...), custom_call_target="tpu_custom_call" | custom-call | flops 671088640 | bytes 3538944 | tf_op jit(solution)/shard_map/far_gradients/pallas_call | solution.py:223
  (255 shorter events, 112.7 us)
Async XLA Ops:
  4.9 16.3 %collective-permute-start = (f32[1,32]{1,0:T(1,128)S(1)}, f32[1,32]{1,0:T(1,128)S(1)}, u32[]{:S(2)}, u32[]{:S(2)}) collective-permute-start(f32[1,32]{1,0:T(1,128)S(1)} %maximum_bitcast_fusion), channel_id=1, source_target_pairs={{0,2},{2,0},{4,6},{6,4},{8,10},{10,8},{12,14},{14,12},{16,18},{18,... | collective-permute-start | bytes 392 | tf_op jit(solution)/shard_map/ppermute | solution.py:340
  16.8 18.0 %collective-permute-start.4 = (f32[2,256,128]{2,1,0:T(8,128)}, f32[2,256,128]{2,1,0:T(8,128)S(1)}, u32[]{:S(2)}, u32[]{:S(2)}) collective-permute-start(f32[2,256,128]{2,1,0:T(8,128)} %get-tuple-element.50), channel_id=1, source_target_pairs={{0,2},{2,0},{4,6},{6,4},{8,10},{10,8},{12,14},{14,12},{16,18},{18,... | collective-permute-start | bytes 786440 | tf_op jit(solution)/shard_map/ppermute | solution.py:372
  16.8 18.0 %collective-permute-start.5 = (f32[2,256,128]{2,1,0:T(8,128)S(1)}, f32[2,256,128]{2,1,0:T(8,128)S(1)}, u32[]{:S(2)}, u32[]{:S(2)}) collective-permute-start(f32[2,256,128]{2,1,0:T(8,128)S(1)} %get-tuple-element.51), channel_id=1, source_target_pairs={{0,4},{2,6},{4,0},{6,2},{8,12},{10,14},{12,8},{14,10},{16,20},{18,... | collective-permute-start | bytes 786440 | tf_op jit(solution)/shard_map/ppermute | solution.py:372
  18.9 15.9 %collective-permute-start.6 = (f32[2,256,128]{2,1,0:T(8,128)S(1)}, f32[2,256,128]{2,1,0:T(8,128)S(1)}, u32[]{:S(2)}, u32[]{:S(2)}) collective-permute-start(f32[2,256,128]{2,1,0:T(8,128)S(1)} %get-tuple-element.52), channel_id=1, source_target_pairs={{0,6},{2,4},{4,2},{6,0},{8,14},{10,12},{12,10},{14,8},{16,22},{18,... | collective-permute-start | bytes 786440 | tf_op jit(solution)/shard_map/ppermute | solution.py:372
  61.6 23.0 %collective-permute-start.11 = (f32[2,256,128]{2,1,0:T(8,128)}, f32[2,256,128]{2,1,0:T(8,128)}, u32[]{:S(2)}, u32[]{:S(2)}) collective-permute-start(f32[2,256,128]{2,1,0:T(8,128)} %get-tuple-element.60), channel_id=1, source_target_pairs={{0,2},{2,0},{4,6},{6,4},{8,10},{10,8},{12,14},{14,12},{16,18},{18,... | collective-permute-start | bytes 786440 | tf_op jit(solution)/shard_map/ppermute | solution.py:372
  68.2 16.4 %collective-permute-start.12 = (f32[2,256,128]{2,1,0:T(8,128)}, f32[2,256,128]{2,1,0:T(8,128)}, u32[]{:S(2)}, u32[]{:S(2)}) collective-permute-start(f32[2,256,128]{2,1,0:T(8,128)} %get-tuple-element.61), channel_id=1, source_target_pairs={{0,4},{2,6},{4,0},{6,2},{8,12},{10,14},{12,8},{14,10},{16,20},{18,... | collective-permute-start | bytes 786440 | tf_op jit(solution)/shard_map/ppermute | solution.py:372
  71.1 13.4 %collective-permute-start.13 = (f32[2,256,128]{2,1,0:T(8,128)}, f32[2,256,128]{2,1,0:T(8,128)}, u32[]{:S(2)}, u32[]{:S(2)}) collective-permute-start(f32[2,256,128]{2,1,0:T(8,128)} %get-tuple-element.62), channel_id=1, source_target_pairs={{0,6},{2,4},{4,2},{6,0},{8,14},{10,12},{12,10},{14,8},{16,22},{18,... | collective-permute-start | bytes 786440 | tf_op jit(solution)/shard_map/ppermute | solution.py:372
  115.1 14.0 %collective-permute-start.43 = (f32[512,256]{1,0:T(8,128)S(1)}, f32[512,256]{1,0:T(8,128)S(1)}, u32[]{:S(2)}, u32[]{:S(2)}) collective-permute-start(f32[512,256]{1,0:T(8,128)S(1)} %dynamic-slice_bitcast_fusion.2), channel_id=1, source_target_pairs={{0,8},{2,10},{4,12},{6,14},{8,0},{10,2},{12,4},{14,6},{16,24},{18,... | collective-permute-start | bytes 1572872 | tf_op jit(solution)/shard_map/ppermute | solution.py:269
  115.1 16.7 %collective-permute-start.15 = (f32[2,256,128]{2,1,0:T(8,128)}, f32[2,256,128]{2,1,0:T(8,128)S(1)}, u32[]{:S(2)}, u32[]{:S(2)}) collective-permute-start(f32[2,256,128]{2,1,0:T(8,128)} %get-tuple-element.69), channel_id=1, source_target_pairs={{0,2},{2,0},{4,6},{6,4},{8,10},{10,8},{12,14},{14,12},{16,18},{18,... | collective-permute-start | bytes 786440 | tf_op jit(solution)/shard_map/ppermute | solution.py:372
  116.6 15.3 %collective-permute-start.16 = (f32[2,256,128]{2,1,0:T(8,128)}, f32[2,256,128]{2,1,0:T(8,128)S(1)}, u32[]{:S(2)}, u32[]{:S(2)}) collective-permute-start(f32[2,256,128]{2,1,0:T(8,128)} %copy-done.32), channel_id=1, source_target_pairs={{0,4},{2,6},{4,0},{6,2},{8,12},{10,14},{12,8},{14,10},{16,20},{18,... | collective-permute-start | bytes 786440 | tf_op jit(solution)/shard_map/ppermute | solution.py:372
  118.6 13.3 %collective-permute-start.17 = (f32[2,256,128]{2,1,0:T(8,128)}, f32[2,256,128]{2,1,0:T(8,128)S(1)}, u32[]{:S(2)}, u32[]{:S(2)}) collective-permute-start(f32[2,256,128]{2,1,0:T(8,128)} %copy-done.31), channel_id=1, source_target_pairs={{0,6},{2,4},{4,2},{6,0},{8,14},{10,12},{12,10},{14,8},{16,22},{18,... | collective-permute-start | bytes 786440 | tf_op jit(solution)/shard_map/ppermute | solution.py:372
  130.9 20.7 %collective-permute-start.44 = (f32[256,256]{1,0:T(8,128)}, f32[256,256]{1,0:T(8,128)}, u32[]{:S(2)}, u32[]{:S(2)}) collective-permute-start(f32[256,256]{1,0:T(8,128)} %dynamic-slice_bitcast_fusion.5), channel_id=1, source_target_pairs={{0,16},{2,18},{4,20},{6,22},{8,24},{10,26},{12,28},{14,30},{16,0},... | collective-permute-start | bytes 786440 | tf_op jit(solution)/shard_map/ppermute | solution.py:269
  135.0 12.8 %collective-permute-start.19 = (f32[256,128]{1,0:T(8,128)S(1)}, f32[256,128]{1,0:T(8,128)S(1)}, u32[]{:S(2)}, u32[]{:S(2)}) collective-permute-start(f32[256,128]{1,0:T(8,128)S(1)} %get-tuple-element.73.refs_1_), channel_id=1, source_target_pairs={{8,0},{10,2},{12,4},{14,6},{16,8},{18,10},{20,12},{22,14},{24,16},... | collective-permute-start | bytes 393224 | tf_op jit(solution)/shard_map/ppermute | solution.py:383
  137.5 27.7 %collective-permute-start.35 = (f32[512,384]{1,0:T(8,128)S(1)}, f32[512,384]{1,0:T(8,128)S(1)}, u32[]{:S(2)}, u32[]{:S(2)}) collective-permute-start(f32[512,384]{1,0:T(8,128)S(1)} %dynamic-slice_bitcast_fusion), channel_id=1, source_target_pairs={{0,4},{2,6},{4,0},{6,2},{8,12},{10,14},{12,8},{14,10},{16,20},{18,... | collective-permute-start | bytes 2359304 | tf_op jit(solution)/shard_map/ppermute | solution.py:269
  154.2 23.2 %collective-permute-start.27 = (f32[512,384]{1,0:T(8,128)S(1)}, f32[512,384]{1,0:T(8,128)S(1)}, u32[]{:S(2)}, u32[]{:S(2)}) collective-permute-start(f32[512,384]{1,0:T(8,128)S(1)} %dynamic-slice_bitcast_fusion.1), channel_id=1, source_target_pairs={{0,2},{2,0},{4,6},{6,4},{8,10},{10,8},{12,14},{14,12},{16,18},{18,... | collective-permute-start | bytes 2359304 | tf_op jit(solution)/shard_map/ppermute | solution.py:269
  161.6 100.8 %collective-permute-start.22 = (f32[2,256,128]{2,1,0:T(8,128)S(1)}, f32[2,256,128]{2,1,0:T(8,128)S(1)}, u32[]{:S(2)}, u32[]{:S(2)}) collective-permute-start(f32[2,256,128]{2,1,0:T(8,128)S(1)} %get-tuple-element.79), channel_id=1, source_target_pairs={{0,2},{2,0},{4,6},{6,4},{8,10},{10,8},{12,14},{14,12},{16,18},{18,... | collective-permute-start | bytes 786440 | tf_op jit(solution)/shard_map/ppermute | solution.py:372
  163.1 109.4 %collective-permute-start.23 = (f32[2,256,128]{2,1,0:T(8,128)S(1)}, f32[2,256,128]{2,1,0:T(8,128)S(1)}, u32[]{:S(2)}, u32[]{:S(2)}) collective-permute-start(f32[2,256,128]{2,1,0:T(8,128)S(1)} %get-tuple-element.80), channel_id=1, source_target_pairs={{0,4},{2,6},{4,0},{6,2},{8,12},{10,14},{12,8},{14,10},{16,20},{18,... | collective-permute-start | bytes 786440 | tf_op jit(solution)/shard_map/ppermute | solution.py:372
  165.2 107.5 %collective-permute-start.24 = (f32[2,256,128]{2,1,0:T(8,128)S(1)}, f32[2,256,128]{2,1,0:T(8,128)S(1)}, u32[]{:S(2)}, u32[]{:S(2)}) collective-permute-start(f32[2,256,128]{2,1,0:T(8,128)S(1)} %get-tuple-element.81), channel_id=1, source_target_pairs={{0,6},{2,4},{4,2},{6,0},{8,14},{10,12},{12,10},{14,8},{16,22},{18,... | collective-permute-start | bytes 786440 | tf_op jit(solution)/shard_map/ppermute | solution.py:372
  177.0 21.9 %collective-permute-start.36 = (f32[256,384]{1,0:T(8,128)S(1)}, f32[256,384]{1,0:T(8,128)S(1)}, u32[]{:S(2)}, u32[]{:S(2)}) collective-permute-start(f32[256,384]{1,0:T(8,128)S(1)} %dynamic-slice_bitcast_fusion.3), channel_id=1, source_target_pairs={{0,2},{2,0},{4,6},{6,4},{8,10},{10,8},{12,14},{14,12},{16,18},{18,... | collective-permute-start | bytes 1179656 | tf_op jit(solution)/shard_map/ppermute | solution.py:269
  177.4 19.7 %collective-permute-start.48 = (f32[128,256]{1,0:T(8,128)S(1)}, f32[128,256]{1,0:T(8,128)S(1)}, u32[]{:S(2)}, u32[]{:S(2)}) collective-permute-start(f32[128,256]{1,0:T(8,128)S(1)} %pad_maximum_fusion.8), channel_id=1, source_target_pairs={{0,2},{2,0},{4,6},{6,4},{8,10},{10,8},{12,14},{14,12},{16,18},{18,... | collective-permute-start | bytes 393224 | tf_op jit(solution)/shard_map/ppermute | solution.py:273
  198.9 26.8 %collective-permute-start.49 = (f32[256,256]{1,0:T(8,128)S(1)}, f32[256,256]{1,0:T(8,128)S(1)}, u32[]{:S(2)}, u32[]{:S(2)}) collective-permute-start(f32[256,256]{1,0:T(8,128)S(1)} %pad_maximum_fusion.5), channel_id=1, source_target_pairs={{0,16},{2,18},{4,20},{6,22},{8,24},{10,26},{12,28},{14,30},{16,0},... | collective-permute-start | bytes 786440 | tf_op jit(solution)/shard_map/ppermute | solution.py:273
  258.3 22.4 %collective-permute-start.50 = (f32[512,256]{1,0:T(8,128)S(1)}, f32[512,256]{1,0:T(8,128)S(1)}, u32[]{:S(2)}, u32[]{:S(2)}) collective-permute-start(f32[512,256]{1,0:T(8,128)S(1)} %pad_maximum_fusion.2), channel_id=1, source_target_pairs={{0,8},{2,10},{4,12},{6,14},{8,0},{10,2},{12,4},{14,6},{16,24},{18,... | collective-permute-start | bytes 1572872 | tf_op jit(solution)/shard_map/ppermute | solution.py:273
  262.0 18.8 %collective-permute-start.42 = (f32[512,384]{1,0:T(8,128)S(1)}, f32[512,384]{1,0:T(8,128)S(1)}, u32[]{:S(2)}, u32[]{:S(2)}) collective-permute-start(f32[512,384]{1,0:T(8,128)S(1)} %pad_maximum_fusion.1), channel_id=1, source_target_pairs={{0,4},{2,6},{4,0},{6,2},{8,12},{10,14},{12,8},{14,10},{16,20},{18,... | collective-permute-start | bytes 2359304 | tf_op jit(solution)/shard_map/ppermute | solution.py:273
  262.4 18.5 %collective-permute-start.34 = (f32[512,384]{1,0:T(8,128)S(1)}, f32[512,384]{1,0:T(8,128)S(1)}, u32[]{:S(2)}, u32[]{:S(2)}) collective-permute-start(f32[512,384]{1,0:T(8,128)S(1)} %pad_maximum_fusion), channel_id=1, source_target_pairs={{0,2},{2,0},{4,6},{6,4},{8,10},{10,8},{12,14},{14,12},{16,18},{18,... | collective-permute-start | bytes 2359304 | tf_op jit(solution)/shard_map/ppermute | solution.py:273
  (62 other events, 711.3 us)

commit v3 on v2

--- a/solution.py
+++ b/solution.py
@@ -260,21 +260,33 @@
     return value
 
 
-def sum_slabs(value, bits):
-    size, me = lax.axis_size("seq"), lax.axis_index("seq")
-    for bit in bits:
-        mine = (me >> bit) & 1
-        halves = value.reshape(2, value.shape[0] // 2, value.shape[1])
-        sent = lax.dynamic_index_in_dim(halves, 1 - mine, 0, keepdims=False)
-        came = lax.ppermute(sent, "seq", [(i, i ^ (1 << bit)) for i in range(size)])
-        value = lax.dynamic_index_in_dim(halves, mine, 0, keepdims=False) + came
-    for bit in reversed(bits):
-        mine = (me >> bit) & 1
-        came = lax.ppermute(value, "seq", [(i, i ^ (1 << bit)) for i in range(size)])
-        first = jnp.where(mine == 0, value, came)
-        second = jnp.where(mine == 0, came, value)
-        value = jnp.concatenate([first, second], axis=0)
-    return value
+def exchange(value, bit):
+    size = lax.axis_size("seq")
+    return lax.ppermute(value, "seq", [(i, i ^ (1 << bit)) for i in range(size)])
+
+
+def sum_slabs(values, orders, beside):
+    me = lax.axis_index("seq")
+    count = len(orders[0])
+    values = list(values)
+    for n in range(count):
+        kept, came = [], []
+        for value, bits in zip(values, orders):
+            mine = (me >> bits[n]) & 1
+            halves = value.reshape(2, value.shape[0] // 2, value.shape[1])
+            kept.append(lax.dynamic_index_in_dim(halves, mine, 0, keepdims=False))
+            came.append(exchange(
+                lax.dynamic_index_in_dim(halves, 1 - mine, 0, keepdims=False), bits[n]))
+        came = beside(n, came)
+        values = [a + b for a, b in zip(kept, came)]
+    for n in reversed(range(count)):
+        came = [exchange(value, bits[n]) for value, bits in zip(values, orders)]
+        came = beside(2 * count - 1 - n, came)
+        for i, (other, bits) in enumerate(zip(came, orders)):
+            first = ((me >> bits[n]) & 1) == 0
+            values[i] = jnp.concatenate(
+                [jnp.where(first, values[i], other), jnp.where(first, other, values[i])], axis=0)
+    return jnp.concatenate(values, axis=1)
 
 
 def factor_reader(factors_ref, quad, heads, steps):
@@ -372,7 +384,7 @@
             lax.ppermute(parts[r], "seq", [(i, i ^ r) for i in range(size)])
             for r in range(1, quad)]
 
-    held = trade(mine)
+    held = yield trade(mine)
     totals = small_call(
         functools.partial(total_kernel, *sizes), "group_totals", factors, held, [one, one])
     sent, before = totals, []
@@ -382,6 +394,7 @@
             shift = sign * quad * 2 ** k
             came.append(lax.ppermute(
                 sent[d], "seq", [(i, i + shift) for i in range(size) if 0 <= i + shift < size]))
+        came = yield came
         if k < steps - 1:
             new = small_call(
                 functools.partial(advance_kernel, *sizes, k), "advance_scan", factors,
@@ -390,7 +403,7 @@
     replies = small_call(
         functools.partial(reply_kernel, *sizes), "group_replies", factors,
         [*held, *came, *before], [both] * quad)
-    return trade(replies)
+    return (yield trade(replies))
 
 
 def body(x_in, gate_in, b_in, c_in, decay_fwd, decay_bwd, skip_gain, norm_gain, w_out, d_out):
@@ -445,13 +458,19 @@
 
     local = call(state_kernel, "local_states", order, (x_in, b_in, cols), [wide, narrow, col],
                  state_out, states, flops=8 * frames * width * state)
-    entry = carry(local, entry_factors, quad, steps)
     near_y, scaled = call(
         within_kernel, "within_slab", order,
         (x_in, b_in, c_in, cols, rows, w_out, d_out, gain, skip),
         [wide, narrow, narrow, col, row, weight_rows, model_rows, lanes, lanes],
         [wide_f32, wide_f32], [wide, wide], [square],
         flops=8 * quad_flops + 2 * frames * width * model)
+    stages = carry(local, entry_factors, quad, steps)
+    flying, at = next(stages), 0
+    while at <= steps:
+        if at == 1:
+            flying, near_y, scaled = lax.optimization_barrier((flying, near_y, scaled))
+        flying, at = stages.send(flying), at + 1
+    entry = flying
     y, sums = call(
         functools.partial(merge_kernel, quad), "merge_entry", order,
         (near_y, scaled, gate_in, c_in, cols, *entry),
@@ -471,23 +490,41 @@
         [wide, wide, *states] + [pl.BlockSpec((PAIR, n), lambda i, p: (p[i], 0)) for n in chunks],
         flops=2 * frames * width * model + 8 * frames * width * state)
     back, local_w = rest[:quad], rest[quad:]
-    exits = carry(back, exit_factors, quad, steps)
-    grad_w = jnp.concatenate(
-        [sum_slabs(part, order) for part, order in zip(local_w, orders)], axis=1)
+    stages = carry(back, exit_factors, quad, steps)
     near_x, near_b, grad_c = call(
         functools.partial(near_kernel, quad), "near_gradients", order,
         (x_in, b_in, c_in, cols, rows, skip, dy, *entry),
         [wide, narrow, narrow, col, row, lanes, wide, *states],
         [wide_f32, narrow_out, narrow_out], [wide, narrow, narrow], [square, square],
         flops=20 * quad_flops)
-    grad_c = sum_over(grad_c, "head")
-    grad_x, grad_b = call(
-        functools.partial(far_kernel, quad), "far_gradients", order,
-        (x_in, b_in, cols, near_x, near_b, *exits),
-        [wide, narrow, col, wide, narrow, *states],
-        [wide_bf16, narrow_out], [wide, narrow], flops=20 * frames * width * state)
-    grad_b = sum_over(grad_b, "head")
-    return grad_x, grad_z, grad_b, grad_c, grad_w
+    held = {"near": (near_x, near_b, grad_c)}
+    last = steps + 1
+
+    def beside(n, came):
+        stage = n - 2
+        if n == 0:
+            came, held["near"] = lax.optimization_barrier((came, held["near"]))
+        elif n == 1:
+            held["c"] = sum_over(held["near"][2], "head")
+            came, held["c"] = lax.optimization_barrier((came, held["c"]))
+        elif stage <= last:
+            flying = held["next"] if stage else next(stages)
+            came, flying = lax.optimization_barrier((came, flying))
+            held["next"] = flying if stage == last else stages.send(flying)
+        elif stage == last + 1:
+            far = call(
+                functools.partial(far_kernel, quad), "far_gradients", order,
+                (x_in, b_in, cols, held["near"][0], held["near"][1], *held["next"]),
+                [wide, narrow, col, wide, narrow, *states],
+                [wide_bf16, narrow_out], [wide, narrow], flops=20 * frames * width * state)
+            came, held["far"] = lax.optimization_barrier((came, far))
+        elif stage == last + 2:
+            held["b"] = sum_over(held["far"][1], "head")
+            came, held["b"] = lax.optimization_barrier((came, held["b"]))
+        return came
+
+    grad_w = sum_slabs(local_w, orders, beside)
+    return held["far"][0], grad_z, held["b"], held["c"], grad_w
 
 
 def solution(mesh):

time: 285 us -> 275 us (0.965)
  waiting for transfers between devices: 122 us -> 79.8 us
  other arithmetic: 14.2 us -> 31 us
  local copies, waits for them, and re-layouts: 21.3 us -> 35.1 us
    ppermute x24, waiting for transfers between devices: 87.5 us -> 62.2 us  [exchange(): return lax.ppermute(value, 'seq', [(i, i ^ 1 << bit) for i in range(size)])]
    ppermute x8, waiting for transfers between devices: 26.9 us -> 2.51 us  [carry(): lax.ppermute(sent[d], 'seq', [(i, i + shift) for i in range(size) if 0 <=...]
    add x12, other arithmetic: 2.44 us -> 11.8 us  [sum_slabs(): values = [a + b for a, b in zip(kept, came)]]
    squeeze x12, local copies, waits for them, and re-layouts: 2.17 us -> 10 us  [sum_slabs(): lax.dynamic_index_in_dim(halves, 1 - mine, 0, keepdims=False)]
    ppermute x12, waiting for transfers between devices: 0.03 us -> 7.29 us  [trade(): lax.ppermute(parts[r], 'seq', [(i, i ^ r) for i in range(size)])]
    unnamed x70 -> x142, local copies, waits for them, and re-layouts: 15 us -> 21 us
    select_n x12, other arithmetic: 0.56 us -> 6.31 us  [sum_slabs(): jnp.where(first, values[i], other)]
    ppermute x24, starting transfers between devices: 23.8 us -> 26.8 us  [exchange(): return lax.ppermute(value, 'seq', [(i, i ^ 1 << bit) for i in range(size)])]
  transfers between devices with their start and end apart: 51 -> 51, of which waited for: 26 -> 26; matrix products, arithmetic and copies ran while one was open for 4% -> 12% of each run, Pallas kernels for 11% -> 11%
where the time goes in v3:
time: 275 us; the launch traced here: 273 us
  waiting for transfers between devices  79.8 us (29%)
  starting transfers between devices  73.7 us (27%)
  Pallas kernels  52.3 us (19%)
  local copies, waits for them, and re-layouts  35.1 us (13%)
  other arithmetic  31 us (11%)
    ppermute x24, waiting for transfers between devices, exchange(): return lax.ppermute(value, 'seq', [(i, i ^ 1 << bit) for i in range(size)])  62.2 us
    pallas_call x6, Pallas kernels, call(): pl.pallas_call(kernel, name=name, grid_spec=pltpu.PrefetchScalarGridSpec(...  47.5 us
    ppermute x24, starting transfers between devices, exchange(): return lax.ppermute(value, 'seq', [(i, i ^ 1 << bit) for i in range(size)])  26.8 us
    unnamed x142, local copies, waits for them, and re-layouts  21 us
    ppermute x12, starting transfers between devices, trade(): lax.ppermute(parts[r], 'seq', [(i, i ^ r) for i in range(size)])  19.2 us
    ppermute x8, starting transfers between devices, carry(): lax.ppermute(sent[d], 'seq', [(i, i + shift) for i in range(size) if 0 <=...  18.6 us
    add x12, other arithmetic, sum_slabs(): values = [a + b for a, b in zip(kept, came)]  11.8 us
    squeeze x12, local copies, waits for them, and re-layouts, sum_slabs(): lax.dynamic_index_in_dim(halves, 1 - mine, 0, keepdims=False)  10 us
  transfers between devices with their start and end apart: 51, of which 26 were waited for; matrix products, arithmetic and copies ran while one was open for 12% of the time, Pallas kernels for 11%

profile of v3, /device:TPU:0, one launch (start us, length us, event | category | flops | bytes accessed | tf_op | source)
XLA Modules:
  0.0 273.4 jit_solution(10917590362308448982)
XLA Ops:
  5.5 2.9 %collective-permute-start = (f32[1,32]{1,0:T(1,128)S(1)}, f32[1,32]{1,0:T(1,128)S(1)}, u32[]{:S(2)}, u32[]{:S(2)}) collective-permute-start(f32[1,32]{1,0:T(1,128)S(1)} %maximum_bitcast_fusion), channel_id=1, source_target_pairs={{0,2},{2,0},{4,6},{6,4},{8,10},{10,8},{12,14},{14,12},{16,18},{18,... | collective-permute-start | bytes 392 | tf_op jit(solution)/shard_map/ppermute | solution.py:352
  11.6 5.8 %local_states.1 = (f32[2,256,128]{2,1,0:T(8,128)S(1)}, f32[2,256,128]{2,1,0:T(8,128)}, f32[2,256,128]{2,1,0:T(8,128)S(1)}, f32[2,256,128]{2,1,0:T(8,128)S(1)}) custom-call(s32[8]{0:T(128)S(1)} %fusion.1.order_ref, bf16[256,1024]{1,0:T(8,128)(2,1)S(1)} %copy-done.4, bf16[256,128]{1,0:T(8,128)(2,1)S(1)} %copy-done.22, f32[8,256,8]{2,1,0:T(8,128)S(1)} %bitcast.98), custom_call_target="tpu_custom_call" | custom-call | flops 268435456 | bytes 1703936 | tf_op jit(solution)/shard_map/local_states/pallas_call | solution.py:223
  37.9 3.6 %collective-permute-start.7 = (f32[256,128]{1,0:T(8,128)S(1)}, f32[256,128]{1,0:T(8,128)S(1)}, u32[]{:S(2)}, u32[]{:S(2)}) collective-permute-start(f32[256,128]{1,0:T(8,128)S(1)} %get-tuple-element.98.refs_0_), channel_id=1, source_target_pairs={{0,8},{2,10},{4,12},{6,14},{8,16},{10,18},{12,20},{14,22},{16,24},... | collective-permute-start | bytes 393224 | tf_op jit(solution)/shard_map/ppermute | solution.py:395
  46.8 8.1 %within_slab.1 = (f32[256,1024]{1,0:T(8,128)S(1)}, f32[256,1024]{1,0:T(8,128)S(1)}) custom-call(s32[8]{0:T(128)S(1)} %copy-done.42, bf16[256,1024]{1,0:T(8,128)(2,1)S(1)} %copy-done.5, bf16[256,128]{1,0:T(8,128)(2,1)S(1)} %copy-done.23, bf16[256,128]{1,0:T(8,128)(2,1)S(1)} %copy-done.21, f32[8,256,8]{2,1,0:T(8,128)S(1)} %bitcast.99, ...), custom_call_target="tpu_custom_call" | custom-call | flops 1610612736 | bytes 5513216 | tf_op jit(solution)/shard_map/within_slab/pallas_call | solution.py:223
  56.8 5.5 %collective-permute-start.9 = (f32[256,128]{1,0:T(8,128)S(1)}, f32[256,128]{1,0:T(8,128)S(1)}, u32[]{:S(2)}, u32[]{:S(2)}) collective-permute-start(f32[256,128]{1,0:T(8,128)S(1)} %get-tuple-element.106), channel_id=1, source_target_pairs={{0,16},{2,18},{4,20},{6,22},{8,24},{10,26},{12,28},{14,30},{1,17},... | collective-permute-start | bytes 393224 | tf_op jit(solution)/shard_map/ppermute | solution.py:395
  65.6 5.6 %collective-permute-start.11 = (f32[2,256,128]{2,1,0:T(8,128)S(1)}, f32[2,256,128]{2,1,0:T(8,128)S(1)}, u32[]{:S(2)}, u32[]{:S(2)}) collective-permute-start(f32[2,256,128]{2,1,0:T(8,128)S(1)} %get-tuple-element.111), channel_id=1, source_target_pairs={{0,2},{2,0},{4,6},{6,4},{8,10},{10,8},{12,14},{14,12},{16,18},{18,... | collective-permute-start | bytes 786440 | tf_op jit(solution)/shard_map/ppermute | solution.py:384
  75.6 4.9 %collective-permute-done.12.refs_2_ = f32[2,256,128]{2,1,0:T(8,128)S(1)} collective-permute-done((f32[2,256,128]{2,1,0:T(8,128)S(1)}, f32[2,256,128]{2,1,0:T(8,128)S(1)}, u32[]{:S(2)}, u32[]{:S(2)}) %collective-permute-start.12) | collective-permute-done | bytes 262176 | tf_op jit(solution)/shard_map/ppermute | solution.py:384
  81.0 5.1 %merge_entry.1 = (f32[256,1024]{1,0:T(8,128)S(1)}, f32[256,2]{1,0:T(8,128)}) custom-call(s32[8]{0:T(128)S(1)} %copy-done.43, f32[256,1024]{1,0:T(8,128)S(1)} %get-tuple-element.102.near_ref, f32[256,1024]{1,0:T(8,128)S(1)} %get-tuple-element.103.m_ref, bf16[256,1024]{1,0:T(8,128)(2,1)S(1)} %copy-done.6, bf16[256,128]{1,0:T(8,128)(2,1)S(1)} %copy-done.21, ...), custom_call_target="tpu_custom_call" | custom-call | flops 268435456 | bytes 4851712 | tf_op jit(solution)/shard_map/merge_entry/pallas_call | solution.py:223
  93.2 12.7 %norm_backward.1 = (f32[256,1024]{1,0:T(8,128)S(1)}, bf16[256,1024]{1,0:T(8,128)(2,1)}, f32[2,256,128]{2,1,0:T(8,128)S(1)}, f32[2,256,128]{2,1,0:T(8,128)}, f32[...) custom-call(s32[8]{0:T(128)S(1)} %copy-done.44, ...), custom_call_target="tpu_custom_call" | custom-call | flops 805306368 | bytes 10098688 | tf_op jit(solution)/shard_map/norm_backward/pallas_call | solution.py:223
  122.0 8.7 %near_gradients.1 = (f32[256,1024]{1,0:T(8,128)S(1)}, f32[256,128]{1,0:T(8,128)S(1)}, f32[256,128]{1,0:T(8,128)}) custom-call(s32[8]{0:T(128)S(1)} %copy-done.45, bf16[256,1024]{1,0:T(8,128)(2,1)S(1)} %copy-done.5, bf16[256,128]{1,0:T(8,128)(2,1)S(1)} %copy-done.23, bf16[256,128]{1,0:T(8,128)(2,1)S(1)} %copy-done.21, f32[8,256,8]{2,1,0:T(8,128)S(1)} %bitcast.102, ...), custom_call_target="tpu_custom_call" | custom-call | flops 2684354560 | bytes 4198400 | tf_op jit(solution)/shard_map/near_gradients/pallas_call | solution.py:223
  142.1 3.4 %collective-permute-start.20 = (f32[256,256]{1,0:T(8,128)S(1)}, f32[256,256]{1,0:T(8,128)S(1)}, u32[]{:S(2)}, u32[]{:S(2)}) collective-permute-start(f32[256,256]{1,0:T(8,128)S(1)} %dynamic-slice_bitcast_fusion.5), channel_id=1, source_target_pairs={{0,16},{2,18},{4,20},{6,22},{8,24},{10,26},{12,28},{14,30},{16,0},... | collective-permute-start | bytes 786440 | tf_op jit(solution)/shard_map/ppermute | solution.py:265
  149.7 6.3 %collective-permute-done.20 = f32[256,256]{1,0:T(8,128)S(1)} collective-permute-done((f32[256,256]{1,0:T(8,128)S(1)}, f32[256,256]{1,0:T(8,128)S(1)}, u32[]{:S(2)}, u32[]{:S(2)}) %collective-permute-start.20) | collective-permute-done | bytes 262176 | tf_op jit(solution)/shard_map/ppermute | solution.py:265
  166.4 4.5 %collective-permute-done.24 = f32[128,256]{1,0:T(8,128)} collective-permute-done((f32[128,256]{1,0:T(8,128)}, f32[128,256]{1,0:T(8,128)}, u32[]{:S(2)}, u32[]{:S(2)}) %collective-permute-start.24) | collective-permute-done | bytes 131104 | tf_op jit(solution)/shard_map/ppermute | solution.py:265
  177.5 4.3 %collective-permute-start.29 = (f32[64,384]{1,0:T(8,128)S(1)}, f32[64,384]{1,0:T(8,128)S(1)}, u32[]{:S(2)}, u32[]{:S(2)}) collective-permute-start(f32[64,384]{1,0:T(8,128)S(1)} %dynamic-slice_bitcast_fusion.9), channel_id=1, source_target_pairs={{0,16},{2,18},{4,20},{6,22},{8,24},{10,26},{12,28},{14,30},{16,0},... | collective-permute-start | bytes 294920 | tf_op jit(solution)/shard_map/ppermute | solution.py:265
  183.5 3.8 %collective-permute-done.30 = f32[64,256]{1,0:T(8,128)S(1)} collective-permute-done((f32[64,256]{1,0:T(8,128)S(1)}, f32[64,256]{1,0:T(8,128)S(1)}, u32[]{:S(2)}, u32[]{:S(2)}) %collective-permute-start.30) | collective-permute-done | bytes 65568 | tf_op jit(solution)/shard_map/ppermute | solution.py:265
  195.4 3.5 %collective-permute-start.34 = (f32[64,384]{1,0:T(8,128)}, f32[64,384]{1,0:T(8,128)}, u32[]{:S(2)}, u32[]{:S(2)}) collective-permute-start(f32[64,384]{1,0:T(8,128)} %bitcast_add_fusion.9), channel_id=1, source_target_pairs={{0,16},{2,18},{4,20},{6,22},{8,24},{10,26},{12,28},{14,30},{16,0},... | collective-permute-start | bytes 294920 | tf_op jit(solution)/shard_map/ppermute | solution.py:265
  200.7 4.1 %collective-permute-done.35 = f32[64,256]{1,0:T(8,128)} collective-permute-done((f32[64,256]{1,0:T(8,128)}, f32[64,256]{1,0:T(8,128)}, u32[]{:S(2)}, u32[]{:S(2)}) %collective-permute-start.35) | collective-permute-done | bytes 65568 | tf_op jit(solution)/shard_map/ppermute | solution.py:265
  204.8 5.9 %collective-permute-done.34 = f32[64,384]{1,0:T(8,128)} collective-permute-done((f32[64,384]{1,0:T(8,128)}, f32[64,384]{1,0:T(8,128)}, u32[]{:S(2)}, u32[]{:S(2)}) %collective-permute-start.34) | collective-permute-done | bytes 98336 | tf_op jit(solution)/shard_map/ppermute | solution.py:265
  223.6 5.7 %collective-permute-done.40 = f32[128,256]{1,0:T(8,128)S(1)} collective-permute-done((f32[128,256]{1,0:T(8,128)S(1)}, f32[128,256]{1,0:T(8,128)S(1)}, u32[]{:S(2)}, u32[]{:S(2)}) %collective-permute-start.40) | collective-permute-done | bytes 131104 | tf_op jit(solution)/shard_map/ppermute | solution.py:265
  230.0 6.0 %collective-permute-done.38 = f32[128,384]{1,0:T(8,128)} collective-permute-done((f32[128,384]{1,0:T(8,128)}, f32[128,384]{1,0:T(8,128)}, u32[]{:S(2)}, u32[]{:S(2)}) %collective-permute-start.38) | collective-permute-done | bytes 196640 | tf_op jit(solution)/shard_map/ppermute | solution.py:265
  240.9 7.0 %far_gradients.1 = (bf16[256,1024]{1,0:T(8,128)(2,1)}, f32[256,128]{1,0:T(8,128)S(1)}) custom-call(s32[8]{0:T(128)S(1)} %copy-done.46, bf16[256,1024]{1,0:T(8,128)(2,1)S(1)} %copy-done.5, bf16[256,128]{1,0:T(8,128)(2,1)S(1)} %copy-done.23, f32[8,256,8]{2,1,0:T(8,128)S(1)} %bitcast.103, f32[256,1024]{1,0:T(8,128)S(1)} %copy-done.16, ...), custom_call_target="tpu_custom_call" | custom-call | flops 671088640 | bytes 3538944 | tf_op jit(solution)/shard_map/far_gradients/pallas_call | solution.py:223
  247.9 3.6 %collective-permute-done.46 = f32[256,256]{1,0:T(8,128)S(1)} collective-permute-done((f32[256,256]{1,0:T(8,128)S(1)}, f32[256,256]{1,0:T(8,128)S(1)}, u32[]{:S(2)}, u32[]{:S(2)}) %collective-permute-start.46) | collective-permute-done | bytes 262176 | tf_op jit(solution)/shard_map/ppermute | solution.py:265
  256.8 9.5 %collective-permute-done.49 = f32[512,256]{1,0:T(8,128)S(1)} collective-permute-done((f32[512,256]{1,0:T(8,128)S(1)}, f32[512,256]{1,0:T(8,128)S(1)}, u32[]{:S(2)}, u32[]{:S(2)}) %collective-permute-start.49) | collective-permute-done | bytes 524320 | tf_op jit(solution)/shard_map/ppermute | solution.py:265
  266.2 3.3 %collective-permute-done.48 = f32[512,384]{1,0:T(8,128)S(1)} collective-permute-done((f32[512,384]{1,0:T(8,128)S(1)}, f32[512,384]{1,0:T(8,128)S(1)}, u32[]{:S(2)}, u32[]{:S(2)}) %collective-permute-start.48) | collective-permute-done | bytes 786464 | tf_op jit(solution)/shard_map/ppermute | solution.py:265
  (327 shorter events, 138.0 us)
Async XLA Ops:
  5.5 16.3 %collective-permute-start = (f32[1,32]{1,0:T(1,128)S(1)}, f32[1,32]{1,0:T(1,128)S(1)}, u32[]{:S(2)}, u32[]{:S(2)}) collective-permute-start(f32[1,32]{1,0:T(1,128)S(1)} %maximum_bitcast_fusion), channel_id=1, source_target_pairs={{0,2},{2,0},{4,6},{6,4},{8,10},{10,8},{12,14},{14,12},{16,18},{18,... | collective-permute-start | bytes 392 | tf_op jit(solution)/shard_map/ppermute | solution.py:352
  17.4 18.4 %collective-permute-start.4 = (f32[2,256,128]{2,1,0:T(8,128)}, f32[2,256,128]{2,1,0:T(8,128)S(1)}, u32[]{:S(2)}, u32[]{:S(2)}) collective-permute-start(f32[2,256,128]{2,1,0:T(8,128)} %get-tuple-element.95), channel_id=1, source_target_pairs={{0,2},{2,0},{4,6},{6,4},{8,10},{10,8},{12,14},{14,12},{16,18},{18,... | collective-permute-start | bytes 786440 | tf_op jit(solution)/shard_map/ppermute | solution.py:384
  17.4 18.4 %collective-permute-start.5 = (f32[2,256,128]{2,1,0:T(8,128)S(1)}, f32[2,256,128]{2,1,0:T(8,128)S(1)}, u32[]{:S(2)}, u32[]{:S(2)}) collective-permute-start(f32[2,256,128]{2,1,0:T(8,128)S(1)} %get-tuple-element.96), channel_id=1, source_target_pairs={{0,4},{2,6},{4,0},{6,2},{8,12},{10,14},{12,8},{14,10},{16,20},{18,... | collective-permute-start | bytes 786440 | tf_op jit(solution)/shard_map/ppermute | solution.py:384
  19.5 16.4 %collective-permute-start.6 = (f32[2,256,128]{2,1,0:T(8,128)S(1)}, f32[2,256,128]{2,1,0:T(8,128)S(1)}, u32[]{:S(2)}, u32[]{:S(2)}) collective-permute-start(f32[2,256,128]{2,1,0:T(8,128)S(1)} %get-tuple-element.97), channel_id=1, source_target_pairs={{0,6},{2,4},{4,2},{6,0},{8,14},{10,12},{12,10},{14,8},{16,22},{18,... | collective-permute-start | bytes 786440 | tf_op jit(solution)/shard_map/ppermute | solution.py:384
  37.9 17.0 %collective-permute-start.7 = (f32[256,128]{1,0:T(8,128)S(1)}, f32[256,128]{1,0:T(8,128)S(1)}, u32[]{:S(2)}, u32[]{:S(2)}) collective-permute-start(f32[256,128]{1,0:T(8,128)S(1)} %get-tuple-element.98.refs_0_), channel_id=1, source_target_pairs={{0,8},{2,10},{4,12},{6,14},{8,16},{10,18},{12,20},{14,22},{16,24},... | collective-permute-start | bytes 393224 | tf_op jit(solution)/shard_map/ppermute | solution.py:395
  111.5 21.2 %collective-permute-start.16 = (f32[512,384]{1,0:T(8,128)}, f32[512,384]{1,0:T(8,128)}, u32[]{:S(2)}, u32[]{:S(2)}) collective-permute-start(f32[512,384]{1,0:T(8,128)} %dynamic-slice_bitcast_fusion), channel_id=1, source_target_pairs={{0,4},{2,6},{4,0},{6,2},{8,12},{10,14},{12,8},{14,10},{16,20},{18,... | collective-permute-start | bytes 2359304 | tf_op jit(solution)/shard_map/ppermute | solution.py:265
  115.5 19.6 %collective-permute-start.15 = (f32[512,384]{1,0:T(8,128)}, f32[512,384]{1,0:T(8,128)}, u32[]{:S(2)}, u32[]{:S(2)}) collective-permute-start(f32[512,384]{1,0:T(8,128)} %dynamic-slice_bitcast_fusion.1), channel_id=1, source_target_pairs={{0,2},{2,0},{4,6},{6,4},{8,10},{10,8},{12,14},{14,12},{16,18},{18,... | collective-permute-start | bytes 2359304 | tf_op jit(solution)/shard_map/ppermute | solution.py:265
  117.9 14.8 %collective-permute-start.17 = (f32[512,256]{1,0:T(8,128)}, f32[512,256]{1,0:T(8,128)}, u32[]{:S(2)}, u32[]{:S(2)}) collective-permute-start(f32[512,256]{1,0:T(8,128)} %dynamic-slice_bitcast_fusion.2), channel_id=1, source_target_pairs={{0,8},{2,10},{4,12},{6,14},{8,0},{10,2},{12,4},{14,6},{16,24},{18,... | collective-permute-start | bytes 1572872 | tf_op jit(solution)/shard_map/ppermute | solution.py:265
  137.3 20.8 %collective-permute-start.19 = (f32[256,384]{1,0:T(8,128)}, f32[256,384]{1,0:T(8,128)}, u32[]{:S(2)}, u32[]{:S(2)}) collective-permute-start(f32[256,384]{1,0:T(8,128)} %dynamic-slice_bitcast_fusion.3), channel_id=1, source_target_pairs={{0,2},{2,0},{4,6},{6,4},{8,10},{10,8},{12,14},{14,12},{16,18},{18,... | collective-permute-start | bytes 1179656 | tf_op jit(solution)/shard_map/ppermute | solution.py:265
  140.0 18.1 %collective-permute-start.18 = (f32[256,384]{1,0:T(8,128)}, f32[256,384]{1,0:T(8,128)}, u32[]{:S(2)}, u32[]{:S(2)}) collective-permute-start(f32[256,384]{1,0:T(8,128)} %dynamic-slice_bitcast_fusion.4), channel_id=1, source_target_pairs={{0,4},{2,6},{4,0},{6,2},{8,12},{10,14},{12,8},{14,10},{16,20},{18,... | collective-permute-start | bytes 1179656 | tf_op jit(solution)/shard_map/ppermute | solution.py:265
  142.1 14.0 %collective-permute-start.20 = (f32[256,256]{1,0:T(8,128)S(1)}, f32[256,256]{1,0:T(8,128)S(1)}, u32[]{:S(2)}, u32[]{:S(2)}) collective-permute-start(f32[256,256]{1,0:T(8,128)S(1)} %dynamic-slice_bitcast_fusion.5), channel_id=1, source_target_pairs={{0,16},{2,18},{4,20},{6,22},{8,24},{10,26},{12,28},{14,30},{16,0},... | collective-permute-start | bytes 786440 | tf_op jit(solution)/shard_map/ppermute | solution.py:265
  145.5 20.1 %collective-permute-start.25 = (f32[2,256,128]{2,1,0:T(8,128)}, f32[2,256,128]{2,1,0:T(8,128)S(1)}, u32[]{:S(2)}, u32[]{:S(2)}) collective-permute-start(f32[2,256,128]{2,1,0:T(8,128)} %get-tuple-element.131), channel_id=1, source_target_pairs={{0,2},{2,0},{4,6},{6,4},{8,10},{10,8},{12,14},{14,12},{16,18},{18,... | collective-permute-start | bytes 786440 | tf_op jit(solution)/shard_map/ppermute | solution.py:384
  147.1 19.3 %collective-permute-start.26 = (f32[2,256,128]{2,1,0:T(8,128)}, f32[2,256,128]{2,1,0:T(8,128)S(1)}, u32[]{:S(2)}, u32[]{:S(2)}) collective-permute-start(f32[2,256,128]{2,1,0:T(8,128)} %copy-done.54), channel_id=1, source_target_pairs={{0,4},{2,6},{4,0},{6,2},{8,12},{10,14},{12,8},{14,10},{16,20},{18,... | collective-permute-start | bytes 786440 | tf_op jit(solution)/shard_map/ppermute | solution.py:384
  171.5 19.6 %collective-permute-start.31 = (f32[256,128]{1,0:T(8,128)S(1)}, f32[256,128]{1,0:T(8,128)S(1)}, u32[]{:S(2)}, u32[]{:S(2)}) collective-permute-start(f32[256,128]{1,0:T(8,128)S(1)} %get-tuple-element.141.refs_0_), channel_id=1, source_target_pairs={{0,8},{2,10},{4,12},{6,14},{8,16},{10,18},{12,20},{14,22},{16,24},... | collective-permute-start | bytes 393224 | tf_op jit(solution)/shard_map/ppermute | solution.py:395
  174.3 16.9 %collective-permute-start.32 = (f32[256,128]{1,0:T(8,128)S(1)}, f32[256,128]{1,0:T(8,128)S(1)}, u32[]{:S(2)}, u32[]{:S(2)}) collective-permute-start(f32[256,128]{1,0:T(8,128)S(1)} %get-tuple-element.142.refs_1_), channel_id=1, source_target_pairs={{8,0},{10,2},{12,4},{14,6},{16,8},{18,10},{20,12},{22,14},{24,16},... | collective-permute-start | bytes 393224 | tf_op jit(solution)/shard_map/ppermute | solution.py:395
  191.8 20.0 %collective-permute-start.36 = (f32[256,128]{1,0:T(8,128)S(1)}, f32[256,128]{1,0:T(8,128)S(1)}, u32[]{:S(2)}, u32[]{:S(2)}) collective-permute-start(f32[256,128]{1,0:T(8,128)S(1)} %get-tuple-element.148), channel_id=1, source_target_pairs={{0,16},{2,18},{4,20},{6,22},{8,24},{10,26},{12,28},{14,30},{1,17},... | collective-permute-start | bytes 393224 | tf_op jit(solution)/shard_map/ppermute | solution.py:395
  193.2 18.5 %collective-permute-start.37 = (f32[256,128]{1,0:T(8,128)S(1)}, f32[256,128]{1,0:T(8,128)S(1)}, u32[]{:S(2)}, u32[]{:S(2)}) collective-permute-start(f32[256,128]{1,0:T(8,128)S(1)} %get-tuple-element.149), channel_id=1, source_target_pairs={{16,0},{18,2},{20,4},{22,6},{24,8},{26,10},{28,12},{30,14},{17,1},... | collective-permute-start | bytes 393224 | tf_op jit(solution)/shard_map/ppermute | solution.py:395
  195.4 15.3 %collective-permute-start.34 = (f32[64,384]{1,0:T(8,128)}, f32[64,384]{1,0:T(8,128)}, u32[]{:S(2)}, u32[]{:S(2)}) collective-permute-start(f32[64,384]{1,0:T(8,128)} %bitcast_add_fusion.9), channel_id=1, source_target_pairs={{0,16},{2,18},{4,20},{6,22},{8,24},{10,26},{12,28},{14,30},{16,0},... | collective-permute-start | bytes 294920 | tf_op jit(solution)/shard_map/ppermute | solution.py:265
  214.0 22.0 %collective-permute-start.41 = (f32[2,256,128]{2,1,0:T(8,128)}, f32[2,256,128]{2,1,0:T(8,128)S(1)}, u32[]{:S(2)}, u32[]{:S(2)}) collective-permute-start(f32[2,256,128]{2,1,0:T(8,128)} %get-tuple-element.158), channel_id=1, source_target_pairs={{0,2},{2,0},{4,6},{6,4},{8,10},{10,8},{12,14},{14,12},{16,18},{18,... | collective-permute-start | bytes 786440 | tf_op jit(solution)/shard_map/ppermute | solution.py:384
  214.6 21.4 %collective-permute-start.42 = (f32[2,256,128]{2,1,0:T(8,128)}, f32[2,256,128]{2,1,0:T(8,128)S(1)}, u32[]{:S(2)}, u32[]{:S(2)}) collective-permute-start(f32[2,256,128]{2,1,0:T(8,128)} %get-tuple-element.159), channel_id=1, source_target_pairs={{0,4},{2,6},{4,0},{6,2},{8,12},{10,14},{12,8},{14,10},{16,20},{18,... | collective-permute-start | bytes 786440 | tf_op jit(solution)/shard_map/ppermute | solution.py:384
  215.5 20.5 %collective-permute-start.43 = (f32[2,256,128]{2,1,0:T(8,128)}, f32[2,256,128]{2,1,0:T(8,128)}, u32[]{:S(2)}, u32[]{:S(2)}) collective-permute-start(f32[2,256,128]{2,1,0:T(8,128)} %get-tuple-element.160), channel_id=1, source_target_pairs={{0,6},{2,4},{4,2},{6,0},{8,14},{10,12},{12,10},{14,8},{16,22},{18,... | collective-permute-start | bytes 786440 | tf_op jit(solution)/shard_map/ppermute | solution.py:384
  237.1 14.4 %collective-permute-start.45 = (f32[256,384]{1,0:T(8,128)S(1)}, f32[256,384]{1,0:T(8,128)S(1)}, u32[]{:S(2)}, u32[]{:S(2)}) collective-permute-start(f32[256,384]{1,0:T(8,128)S(1)} %pad_maximum_fusion.4), channel_id=1, source_target_pairs={{0,2},{2,0},{4,6},{6,4},{8,10},{10,8},{12,14},{14,12},{16,18},{18,... | collective-permute-start | bytes 1179656 | tf_op jit(solution)/shard_map/ppermute | solution.py:265
  251.7 17.8 %collective-permute-start.48 = (f32[512,384]{1,0:T(8,128)S(1)}, f32[512,384]{1,0:T(8,128)S(1)}, u32[]{:S(2)}, u32[]{:S(2)}) collective-permute-start(f32[512,384]{1,0:T(8,128)S(1)} %pad_maximum_fusion.1), channel_id=1, source_target_pairs={{0,4},{2,6},{4,0},{6,2},{8,12},{10,14},{12,8},{14,10},{16,20},{18,... | collective-permute-start | bytes 2359304 | tf_op jit(solution)/shard_map/ppermute | solution.py:265
  253.0 17.5 %collective-permute-start.47 = (f32[512,384]{1,0:T(8,128)S(1)}, f32[512,384]{1,0:T(8,128)S(1)}, u32[]{:S(2)}, u32[]{:S(2)}) collective-permute-start(f32[512,384]{1,0:T(8,128)S(1)} %pad_maximum_fusion), channel_id=1, source_target_pairs={{0,2},{2,0},{4,6},{6,4},{8,10},{10,8},{12,14},{14,12},{16,18},{18,... | collective-permute-start | bytes 2359304 | tf_op jit(solution)/shard_map/ppermute | solution.py:265
  (98 other events, 1055.5 us)

commit v4 on v3

--- a/solution.py
+++ b/solution.py
@@ -279,7 +279,13 @@
                 lax.dynamic_index_in_dim(halves, 1 - mine, 0, keepdims=False), bits[n]))
         came = beside(n, came)
         values = [a + b for a, b in zip(kept, came)]
+        if n == 1:
+            values = [jnp.concatenate(values[:2], axis=1), values[2]]
+            all_orders, orders = orders, orders[1:]
     for n in reversed(range(count)):
+        if n == 1:
+            values = [*jnp.split(values[0], 2, axis=1), values[1]]
+            orders = all_orders
         came = [exchange(value, bits[n]) for value, bits in zip(values, orders)]
         came = beside(2 * count - 1 - n, came)
         for i, (other, bits) in enumerate(zip(came, orders)):

time: 275 us -> 267 us (0.971)
  waiting for transfers between devices: 79.8 us -> 72.4 us
  other arithmetic: 31 us -> 27.6 us
    ppermute x24 -> x20, waiting for transfers between devices: 62.2 us -> 50.8 us  [exchange(): return lax.ppermute(value, 'seq', [(i, i ^ 1 << bit) for i in range(size)])]
    ppermute x8, waiting for transfers between devices: 2.51 us -> 6.57 us  [carry(): lax.ppermute(sent[d], 'seq', [(i, i + shift) for i in range(size) if 0 <=...]
    select_n x12 -> x9, other arithmetic: 6.31 us -> 3.31 us  [sum_slabs(): jnp.where(first, values[i], other)]
    add x12 -> x10, other arithmetic: 11.8 us -> 10.3 us  [sum_slabs(): values = [a + b for a, b in zip(kept, came)]]
    ppermute x24 -> x20, starting transfers between devices: 26.8 us -> 28.2 us  [exchange(): return lax.ppermute(value, 'seq', [(i, i ^ 1 << bit) for i in range(size)])]
    squeeze x12 -> x10, local copies, waits for them, and re-layouts: 10 us -> 9.37 us  [sum_slabs(): lax.dynamic_index_in_dim(halves, 1 - mine, 0, keepdims=False)]
    unnamed x142 -> x138, local copies, waits for them, and re-layouts: 21 us -> 21 us
  transfers between devices with their start and end apart: 51 -> 47, of which waited for: 26 -> 26; matrix products, arithmetic and copies ran while one was open for 12% -> 10% of each run, Pallas kernels for 11% -> 11%
where the time goes in v4:
time: 267 us; the launch traced here: 264 us
  starting transfers between devices  76 us (28%)
  waiting for transfers between devices  72.4 us (27%)
  Pallas kernels  52.3 us (20%)
  local copies, waits for them, and re-layouts  34.4 us (13%)
  other arithmetic  27.6 us (10%)
    ppermute x20, waiting for transfers between devices, exchange(): return lax.ppermute(value, 'seq', [(i, i ^ 1 << bit) for i in range(size)])  50.8 us
    pallas_call x6, Pallas kernels, call(): pl.pallas_call(kernel, name=name, grid_spec=pltpu.PrefetchScalarGridSpec(...  47.5 us
    ppermute x20, starting transfers between devices, exchange(): return lax.ppermute(value, 'seq', [(i, i ^ 1 << bit) for i in range(size)])  28.2 us
    unnamed x138, local copies, waits for them, and re-layouts  21 us
    ppermute x8, starting transfers between devices, carry(): lax.ppermute(sent[d], 'seq', [(i, i + shift) for i in range(size) if 0 <=...  19.5 us
    ppermute x12, starting transfers between devices, trade(): lax.ppermute(parts[r], 'seq', [(i, i ^ r) for i in range(size)])  19.2 us
    add x10, other arithmetic, sum_slabs(): values = [a + b for a, b in zip(kept, came)]  10.3 us
    squeeze x10, local copies, waits for them, and re-layouts, sum_slabs(): lax.dynamic_index_in_dim(halves, 1 - mine, 0, keepdims=False)  9.37 us
  transfers between devices with their start and end apart: 47, of which 26 were waited for; matrix products, arithmetic and copies ran while one was open for 10% of the time, Pallas kernels for 11%

profile of v4, /device:TPU:0, one launch (start us, length us, event | category | flops | bytes accessed | tf_op | source)
XLA Modules:
  0.0 264.3 jit_solution(7706568637111099393)
XLA Ops:
  5.5 2.9 %collective-permute-start = (f32[1,32]{1,0:T(1,128)S(1)}, f32[1,32]{1,0:T(1,128)S(1)}, u32[]{:S(2)}, u32[]{:S(2)}) collective-permute-start(f32[1,32]{1,0:T(1,128)S(1)} %maximum_bitcast_fusion), channel_id=1, source_target_pairs={{0,2},{2,0},{4,6},{6,4},{8,10},{10,8},{12,14},{14,12},{16,18},{18,... | collective-permute-start | bytes 392 | tf_op jit(solution)/shard_map/ppermute | solution.py:358
  11.6 5.8 %local_states.1 = (f32[2,256,128]{2,1,0:T(8,128)S(1)}, f32[2,256,128]{2,1,0:T(8,128)}, f32[2,256,128]{2,1,0:T(8,128)S(1)}, f32[2,256,128]{2,1,0:T(8,128)S(1)}) custom-call(s32[8]{0:T(128)S(1)} %fusion.2.order_ref, bf16[256,1024]{1,0:T(8,128)(2,1)S(1)} %copy-done.4, bf16[256,128]{1,0:T(8,128)(2,1)S(1)} %copy-done.22, f32[8,256,8]{2,1,0:T(8,128)S(1)} %bitcast.88), custom_call_target="tpu_custom_call" | custom-call | flops 268435456 | bytes 1703936 | tf_op jit(solution)/shard_map/local_states/pallas_call | solution.py:223
  37.9 3.6 %collective-permute-start.7 = (f32[256,128]{1,0:T(8,128)S(1)}, f32[256,128]{1,0:T(8,128)S(1)}, u32[]{:S(2)}, u32[]{:S(2)}) collective-permute-start(f32[256,128]{1,0:T(8,128)S(1)} %get-tuple-element.94.refs_0_), channel_id=1, source_target_pairs={{0,8},{2,10},{4,12},{6,14},{8,16},{10,18},{12,20},{14,22},{16,24},... | collective-permute-start | bytes 393224 | tf_op jit(solution)/shard_map/ppermute | solution.py:401
  46.7 8.1 %within_slab.1 = (f32[256,1024]{1,0:T(8,128)S(1)}, f32[256,1024]{1,0:T(8,128)S(1)}) custom-call(s32[8]{0:T(128)S(1)} %copy-done.42, bf16[256,1024]{1,0:T(8,128)(2,1)S(1)} %copy-done.5, bf16[256,128]{1,0:T(8,128)(2,1)S(1)} %copy-done.23, bf16[256,128]{1,0:T(8,128)(2,1)S(1)} %copy-done.21, f32[8,256,8]{2,1,0:T(8,128)S(1)} %bitcast.89, ...), custom_call_target="tpu_custom_call" | custom-call | flops 1610612736 | bytes 5513216 | tf_op jit(solution)/shard_map/within_slab/pallas_call | solution.py:223
  56.8 5.5 %collective-permute-start.9 = (f32[256,128]{1,0:T(8,128)S(1)}, f32[256,128]{1,0:T(8,128)S(1)}, u32[]{:S(2)}, u32[]{:S(2)}) collective-permute-start(f32[256,128]{1,0:T(8,128)S(1)} %get-tuple-element.102), channel_id=1, source_target_pairs={{0,16},{2,18},{4,20},{6,22},{8,24},{10,26},{12,28},{14,30},{1,17},... | collective-permute-start | bytes 393224 | tf_op jit(solution)/shard_map/ppermute | solution.py:401
  65.6 5.6 %collective-permute-start.11 = (f32[2,256,128]{2,1,0:T(8,128)S(1)}, f32[2,256,128]{2,1,0:T(8,128)S(1)}, u32[]{:S(2)}, u32[]{:S(2)}) collective-permute-start(f32[2,256,128]{2,1,0:T(8,128)S(1)} %get-tuple-element.107), channel_id=1, source_target_pairs={{0,2},{2,0},{4,6},{6,4},{8,10},{10,8},{12,14},{14,12},{16,18},{18,... | collective-permute-start | bytes 786440 | tf_op jit(solution)/shard_map/ppermute | solution.py:390
  75.6 4.9 %collective-permute-done.12.refs_2_ = f32[2,256,128]{2,1,0:T(8,128)S(1)} collective-permute-done((f32[2,256,128]{2,1,0:T(8,128)S(1)}, f32[2,256,128]{2,1,0:T(8,128)S(1)}, u32[]{:S(2)}, u32[]{:S(2)}) %collective-permute-start.12) | collective-permute-done | bytes 262176 | tf_op jit(solution)/shard_map/ppermute | solution.py:390
  81.0 5.1 %merge_entry.1 = (f32[256,1024]{1,0:T(8,128)S(1)}, f32[256,2]{1,0:T(8,128)}) custom-call(s32[8]{0:T(128)S(1)} %copy-done.43, f32[256,1024]{1,0:T(8,128)S(1)} %get-tuple-element.98.near_ref, f32[256,1024]{1,0:T(8,128)S(1)} %get-tuple-element.99.m_ref, bf16[256,1024]{1,0:T(8,128)(2,1)S(1)} %copy-done.6, bf16[256,128]{1,0:T(8,128)(2,1)S(1)} %copy-done.21, ...), custom_call_target="tpu_custom_call" | custom-call | flops 268435456 | bytes 4851712 | tf_op jit(solution)/shard_map/merge_entry/pallas_call | solution.py:223
  93.2 12.7 %norm_backward.1 = (f32[256,1024]{1,0:T(8,128)S(1)}, bf16[256,1024]{1,0:T(8,128)(2,1)}, f32[2,256,128]{2,1,0:T(8,128)S(1)}, f32[2,256,128]{2,1,0:T(8,128)}, f32[...) custom-call(s32[8]{0:T(128)S(1)} %copy-done.44, ...), custom_call_target="tpu_custom_call" | custom-call | flops 805306368 | bytes 10098688 | tf_op jit(solution)/shard_map/norm_backward/pallas_call | solution.py:223
  122.0 8.7 %near_gradients.1 = (f32[256,1024]{1,0:T(8,128)S(1)}, f32[256,128]{1,0:T(8,128)S(1)}, f32[256,128]{1,0:T(8,128)}) custom-call(s32[8]{0:T(128)S(1)} %copy-done.45, bf16[256,1024]{1,0:T(8,128)(2,1)S(1)} %copy-done.5, bf16[256,128]{1,0:T(8,128)(2,1)S(1)} %copy-done.23, bf16[256,128]{1,0:T(8,128)(2,1)S(1)} %copy-done.21, f32[8,256,8]{2,1,0:T(8,128)S(1)} %bitcast.92, ...), custom_call_target="tpu_custom_call" | custom-call | flops 2684354560 | bytes 4198400 | tf_op jit(solution)/shard_map/near_gradients/pallas_call | solution.py:223
  142.0 3.4 %collective-permute-start.20 = (f32[256,256]{1,0:T(8,128)S(1)}, f32[256,256]{1,0:T(8,128)S(1)}, u32[]{:S(2)}, u32[]{:S(2)}) collective-permute-start(f32[256,256]{1,0:T(8,128)S(1)} %dynamic-slice_bitcast_fusion.6), channel_id=1, source_target_pairs={{0,16},{2,18},{4,20},{6,22},{8,24},{10,26},{12,28},{14,30},{16,0},... | collective-permute-start | bytes 786440 | tf_op jit(solution)/shard_map/ppermute | solution.py:265
  149.7 6.2 %collective-permute-done.20 = f32[256,256]{1,0:T(8,128)S(1)} collective-permute-done((f32[256,256]{1,0:T(8,128)S(1)}, f32[256,256]{1,0:T(8,128)S(1)}, u32[]{:S(2)}, u32[]{:S(2)}) %collective-permute-start.20) | collective-permute-done | bytes 262176 | tf_op jit(solution)/shard_map/ppermute | solution.py:265
  165.1 4.4 %collective-permute-done.23 = f32[128,256]{1,0:T(8,128)} collective-permute-done((f32[128,256]{1,0:T(8,128)}, f32[128,256]{1,0:T(8,128)}, u32[]{:S(2)}, u32[]{:S(2)}) %collective-permute-start.23) | collective-permute-done | bytes 131104 | tf_op jit(solution)/shard_map/ppermute | solution.py:265
  171.9 3.7 %collective-permute-start.29 = (f32[256,128]{1,0:T(8,128)S(1)}, f32[256,128]{1,0:T(8,128)S(1)}, u32[]{:S(2)}, u32[]{:S(2)}) collective-permute-start(f32[256,128]{1,0:T(8,128)S(1)} %get-tuple-element.136.refs_0_), channel_id=1, source_target_pairs={{0,8},{2,10},{4,12},{6,14},{8,16},{10,18},{12,20},{14,22},{16,24},... | collective-permute-start | bytes 393224 | tf_op jit(solution)/shard_map/ppermute | solution.py:401
  177.9 4.3 %collective-permute-start.27 = (f32[64,768]{1,0:T(8,128)S(1)}, f32[64,768]{1,0:T(8,128)S(1)}, u32[]{:S(2)}, u32[]{:S(2)}) collective-permute-start(f32[64,768]{1,0:T(8,128)S(1)} %dynamic-slice_bitcast_fusion.7), channel_id=1, source_target_pairs={{0,16},{2,18},{4,20},{6,22},{8,24},{10,26},{12,28},{14,30},{16,0},... | collective-permute-start | bytes 589832 | tf_op jit(solution)/shard_map/ppermute | solution.py:265
  183.8 3.8 %collective-permute-done.28 = f32[64,256]{1,0:T(8,128)S(1)} collective-permute-done((f32[64,256]{1,0:T(8,128)S(1)}, f32[64,256]{1,0:T(8,128)S(1)}, u32[]{:S(2)}, u32[]{:S(2)}) %collective-permute-start.28) | collective-permute-done | bytes 65568 | tf_op jit(solution)/shard_map/ppermute | solution.py:265
  187.6 4.2 %collective-permute-done.27 = f32[64,768]{1,0:T(8,128)S(1)} collective-permute-done((f32[64,768]{1,0:T(8,128)S(1)}, f32[64,768]{1,0:T(8,128)S(1)}, u32[]{:S(2)}, u32[]{:S(2)}) %collective-permute-start.27) | collective-permute-done | bytes 196640 | tf_op jit(solution)/shard_map/ppermute | solution.py:265
  196.0 3.5 %collective-permute-start.31 = (f32[64,768]{1,0:T(8,128)}, f32[64,768]{1,0:T(8,128)}, u32[]{:S(2)}, u32[]{:S(2)}) collective-permute-start(f32[64,768]{1,0:T(8,128)} %bitcast_add_fusion.7), channel_id=1, source_target_pairs={{0,16},{2,18},{4,20},{6,22},{8,24},{10,26},{12,28},{14,30},{16,0},... | collective-permute-start | bytes 589832 | tf_op jit(solution)/shard_map/ppermute | solution.py:265
  200.7 4.1 %collective-permute-done.32 = f32[64,256]{1,0:T(8,128)} collective-permute-done((f32[64,256]{1,0:T(8,128)}, f32[64,256]{1,0:T(8,128)}, u32[]{:S(2)}, u32[]{:S(2)}) %collective-permute-start.32) | collective-permute-done | bytes 65568 | tf_op jit(solution)/shard_map/ppermute | solution.py:265
  204.8 4.1 %collective-permute-done.34.refs_5_ = f32[256,128]{1,0:T(8,128)S(1)} collective-permute-done((f32[256,128]{1,0:T(8,128)S(1)}, f32[256,128]{1,0:T(8,128)S(1)}, u32[]{:S(2)}, u32[]{:S(2)}) %collective-permute-start.34) | collective-permute-done | bytes 131104 | tf_op jit(solution)/shard_map/ppermute | solution.py:401
  222.1 4.7 %collective-permute-done.36 = f32[128,256]{1,0:T(8,128)} collective-permute-done((f32[128,256]{1,0:T(8,128)}, f32[128,256]{1,0:T(8,128)}, u32[]{:S(2)}, u32[]{:S(2)}) %collective-permute-start.36) | collective-permute-done | bytes 131104 | tf_op jit(solution)/shard_map/ppermute | solution.py:265
  233.4 7.0 %far_gradients.1 = (bf16[256,1024]{1,0:T(8,128)(2,1)}, f32[256,128]{1,0:T(8,128)S(1)}) custom-call(s32[8]{0:T(128)S(1)} %copy-done.46, bf16[256,1024]{1,0:T(8,128)(2,1)S(1)} %copy-done.5, bf16[256,128]{1,0:T(8,128)(2,1)S(1)} %copy-done.23, f32[8,256,8]{2,1,0:T(8,128)S(1)} %bitcast.93, f32[256,1024]{1,0:T(8,128)S(1)} %copy-done.16, ...), custom_call_target="tpu_custom_call" | custom-call | flops 671088640 | bytes 3538944 | tf_op jit(solution)/shard_map/far_gradients/pallas_call | solution.py:223
  240.4 2.9 %collective-permute-done.42 = f32[256,256]{1,0:T(8,128)S(1)} collective-permute-done((f32[256,256]{1,0:T(8,128)S(1)}, f32[256,256]{1,0:T(8,128)S(1)}, u32[]{:S(2)}, u32[]{:S(2)}) %collective-permute-start.42) | collective-permute-done | bytes 262176 | tf_op jit(solution)/shard_map/ppermute | solution.py:265
  249.1 9.3 %collective-permute-done.45 = f32[512,256]{1,0:T(8,128)S(1)} collective-permute-done((f32[512,256]{1,0:T(8,128)S(1)}, f32[512,256]{1,0:T(8,128)S(1)}, u32[]{:S(2)}, u32[]{:S(2)}) %collective-permute-start.45) | collective-permute-done | bytes 524320 | tf_op jit(solution)/shard_map/ppermute | solution.py:265
  (308 shorter events, 134.3 us)
Async XLA Ops:
  5.5 16.3 %collective-permute-start = (f32[1,32]{1,0:T(1,128)S(1)}, f32[1,32]{1,0:T(1,128)S(1)}, u32[]{:S(2)}, u32[]{:S(2)}) collective-permute-start(f32[1,32]{1,0:T(1,128)S(1)} %maximum_bitcast_fusion), channel_id=1, source_target_pairs={{0,2},{2,0},{4,6},{6,4},{8,10},{10,8},{12,14},{14,12},{16,18},{18,... | collective-permute-start | bytes 392 | tf_op jit(solution)/shard_map/ppermute | solution.py:358
  17.4 18.4 %collective-permute-start.4 = (f32[2,256,128]{2,1,0:T(8,128)}, f32[2,256,128]{2,1,0:T(8,128)S(1)}, u32[]{:S(2)}, u32[]{:S(2)}) collective-permute-start(f32[2,256,128]{2,1,0:T(8,128)} %get-tuple-element.91), channel_id=1, source_target_pairs={{0,2},{2,0},{4,6},{6,4},{8,10},{10,8},{12,14},{14,12},{16,18},{18,... | collective-permute-start | bytes 786440 | tf_op jit(solution)/shard_map/ppermute | solution.py:390
  17.4 18.4 %collective-permute-start.5 = (f32[2,256,128]{2,1,0:T(8,128)S(1)}, f32[2,256,128]{2,1,0:T(8,128)S(1)}, u32[]{:S(2)}, u32[]{:S(2)}) collective-permute-start(f32[2,256,128]{2,1,0:T(8,128)S(1)} %get-tuple-element.92), channel_id=1, source_target_pairs={{0,4},{2,6},{4,0},{6,2},{8,12},{10,14},{12,8},{14,10},{16,20},{18,... | collective-permute-start | bytes 786440 | tf_op jit(solution)/shard_map/ppermute | solution.py:390
  19.5 16.4 %collective-permute-start.6 = (f32[2,256,128]{2,1,0:T(8,128)S(1)}, f32[2,256,128]{2,1,0:T(8,128)S(1)}, u32[]{:S(2)}, u32[]{:S(2)}) collective-permute-start(f32[2,256,128]{2,1,0:T(8,128)S(1)} %get-tuple-element.93), channel_id=1, source_target_pairs={{0,6},{2,4},{4,2},{6,0},{8,14},{10,12},{12,10},{14,8},{16,22},{18,... | collective-permute-start | bytes 786440 | tf_op jit(solution)/shard_map/ppermute | solution.py:390
  37.9 17.0 %collective-permute-start.7 = (f32[256,128]{1,0:T(8,128)S(1)}, f32[256,128]{1,0:T(8,128)S(1)}, u32[]{:S(2)}, u32[]{:S(2)}) collective-permute-start(f32[256,128]{1,0:T(8,128)S(1)} %get-tuple-element.94.refs_0_), channel_id=1, source_target_pairs={{0,8},{2,10},{4,12},{6,14},{8,16},{10,18},{12,20},{14,22},{16,24},... | collective-permute-start | bytes 393224 | tf_op jit(solution)/shard_map/ppermute | solution.py:401
  41.5 13.3 %collective-permute-start.8 = (f32[256,128]{1,0:T(8,128)S(1)}, f32[256,128]{1,0:T(8,128)S(1)}, u32[]{:S(2)}, u32[]{:S(2)}) collective-permute-start(f32[256,128]{1,0:T(8,128)S(1)} %get-tuple-element.95.refs_1_), channel_id=1, source_target_pairs={{8,0},{10,2},{12,4},{14,6},{16,8},{18,10},{20,12},{22,14},{24,16},... | collective-permute-start | bytes 393224 | tf_op jit(solution)/shard_map/ppermute | solution.py:401
  111.4 21.3 %collective-permute-start.16 = (f32[512,384]{1,0:T(8,128)}, f32[512,384]{1,0:T(8,128)}, u32[]{:S(2)}, u32[]{:S(2)}) collective-permute-start(f32[512,384]{1,0:T(8,128)} %dynamic-slice_bitcast_fusion), channel_id=1, source_target_pairs={{0,4},{2,6},{4,0},{6,2},{8,12},{10,14},{12,8},{14,10},{16,20},{18,... | collective-permute-start | bytes 2359304 | tf_op jit(solution)/shard_map/ppermute | solution.py:265
  115.5 19.6 %collective-permute-start.15 = (f32[512,384]{1,0:T(8,128)}, f32[512,384]{1,0:T(8,128)}, u32[]{:S(2)}, u32[]{:S(2)}) collective-permute-start(f32[512,384]{1,0:T(8,128)} %dynamic-slice_bitcast_fusion.1), channel_id=1, source_target_pairs={{0,2},{2,0},{4,6},{6,4},{8,10},{10,8},{12,14},{14,12},{16,18},{18,... | collective-permute-start | bytes 2359304 | tf_op jit(solution)/shard_map/ppermute | solution.py:265
  117.9 14.8 %collective-permute-start.17 = (f32[512,256]{1,0:T(8,128)}, f32[512,256]{1,0:T(8,128)}, u32[]{:S(2)}, u32[]{:S(2)}) collective-permute-start(f32[512,256]{1,0:T(8,128)} %dynamic-slice_bitcast_fusion.2), channel_id=1, source_target_pairs={{0,8},{2,10},{4,12},{6,14},{8,0},{10,2},{12,4},{14,6},{16,24},{18,... | collective-permute-start | bytes 1572872 | tf_op jit(solution)/shard_map/ppermute | solution.py:265
  137.2 20.8 %collective-permute-start.19 = (f32[256,384]{1,0:T(8,128)}, f32[256,384]{1,0:T(8,128)}, u32[]{:S(2)}, u32[]{:S(2)}) collective-permute-start(f32[256,384]{1,0:T(8,128)} %dynamic-slice_bitcast_fusion.4), channel_id=1, source_target_pairs={{0,2},{2,0},{4,6},{6,4},{8,10},{10,8},{12,14},{14,12},{16,18},{18,... | collective-permute-start | bytes 1179656 | tf_op jit(solution)/shard_map/ppermute | solution.py:265
  139.9 18.1 %collective-permute-start.18 = (f32[256,384]{1,0:T(8,128)}, f32[256,384]{1,0:T(8,128)}, u32[]{:S(2)}, u32[]{:S(2)}) collective-permute-start(f32[256,384]{1,0:T(8,128)} %dynamic-slice_bitcast_fusion.5), channel_id=1, source_target_pairs={{0,4},{2,6},{4,0},{6,2},{8,12},{10,14},{12,8},{14,10},{16,20},{18,... | collective-permute-start | bytes 1179656 | tf_op jit(solution)/shard_map/ppermute | solution.py:265
  142.0 14.0 %collective-permute-start.20 = (f32[256,256]{1,0:T(8,128)S(1)}, f32[256,256]{1,0:T(8,128)S(1)}, u32[]{:S(2)}, u32[]{:S(2)}) collective-permute-start(f32[256,256]{1,0:T(8,128)S(1)} %dynamic-slice_bitcast_fusion.6), channel_id=1, source_target_pairs={{0,16},{2,18},{4,20},{6,22},{8,24},{10,26},{12,28},{14,30},{16,0},... | collective-permute-start | bytes 786440 | tf_op jit(solution)/shard_map/ppermute | solution.py:265
  145.4 19.6 %collective-permute-start.24 = (f32[2,256,128]{2,1,0:T(8,128)}, f32[2,256,128]{2,1,0:T(8,128)S(1)}, u32[]{:S(2)}, u32[]{:S(2)}) collective-permute-start(f32[2,256,128]{2,1,0:T(8,128)} %get-tuple-element.127), channel_id=1, source_target_pairs={{0,2},{2,0},{4,6},{6,4},{8,10},{10,8},{12,14},{14,12},{16,18},{18,... | collective-permute-start | bytes 786440 | tf_op jit(solution)/shard_map/ppermute | solution.py:390
  147.0 18.1 %collective-permute-start.25 = (f32[2,256,128]{2,1,0:T(8,128)}, f32[2,256,128]{2,1,0:T(8,128)S(1)}, u32[]{:S(2)}, u32[]{:S(2)}) collective-permute-start(f32[2,256,128]{2,1,0:T(8,128)} %copy-done.54), channel_id=1, source_target_pairs={{0,4},{2,6},{4,0},{6,2},{8,12},{10,14},{12,8},{14,10},{16,20},{18,... | collective-permute-start | bytes 786440 | tf_op jit(solution)/shard_map/ppermute | solution.py:390
  171.9 15.7 %collective-permute-start.29 = (f32[256,128]{1,0:T(8,128)S(1)}, f32[256,128]{1,0:T(8,128)S(1)}, u32[]{:S(2)}, u32[]{:S(2)}) collective-permute-start(f32[256,128]{1,0:T(8,128)S(1)} %get-tuple-element.136.refs_0_), channel_id=1, source_target_pairs={{0,8},{2,10},{4,12},{6,14},{8,16},{10,18},{12,20},{14,22},{16,24},... | collective-permute-start | bytes 393224 | tf_op jit(solution)/shard_map/ppermute | solution.py:401
  177.9 13.9 %collective-permute-start.27 = (f32[64,768]{1,0:T(8,128)S(1)}, f32[64,768]{1,0:T(8,128)S(1)}, u32[]{:S(2)}, u32[]{:S(2)}) collective-permute-start(f32[64,768]{1,0:T(8,128)S(1)} %dynamic-slice_bitcast_fusion.7), channel_id=1, source_target_pairs={{0,16},{2,18},{4,20},{6,22},{8,24},{10,26},{12,28},{14,30},{16,0},... | collective-permute-start | bytes 589832 | tf_op jit(solution)/shard_map/ppermute | solution.py:265
  193.8 15.0 %collective-permute-start.34 = (f32[256,128]{1,0:T(8,128)S(1)}, f32[256,128]{1,0:T(8,128)S(1)}, u32[]{:S(2)}, u32[]{:S(2)}) collective-permute-start(f32[256,128]{1,0:T(8,128)S(1)} %get-tuple-element.143), channel_id=1, source_target_pairs={{16,0},{18,2},{20,4},{22,6},{24,8},{26,10},{28,12},{30,14},{17,1},... | collective-permute-start | bytes 393224 | tf_op jit(solution)/shard_map/ppermute | solution.py:401
  196.0 15.0 %collective-permute-start.31 = (f32[64,768]{1,0:T(8,128)}, f32[64,768]{1,0:T(8,128)}, u32[]{:S(2)}, u32[]{:S(2)}) collective-permute-start(f32[64,768]{1,0:T(8,128)} %bitcast_add_fusion.7), channel_id=1, source_target_pairs={{0,16},{2,18},{4,20},{6,22},{8,24},{10,26},{12,28},{14,30},{16,0},... | collective-permute-start | bytes 589832 | tf_op jit(solution)/shard_map/ppermute | solution.py:265
  213.3 13.5 %collective-permute-start.37 = (f32[2,256,128]{2,1,0:T(8,128)}, f32[2,256,128]{2,1,0:T(8,128)S(1)}, u32[]{:S(2)}, u32[]{:S(2)}) collective-permute-start(f32[2,256,128]{2,1,0:T(8,128)} %get-tuple-element.151), channel_id=1, source_target_pairs={{0,2},{2,0},{4,6},{6,4},{8,10},{10,8},{12,14},{14,12},{16,18},{18,... | collective-permute-start | bytes 786440 | tf_op jit(solution)/shard_map/ppermute | solution.py:390
  213.9 12.9 %collective-permute-start.38 = (f32[2,256,128]{2,1,0:T(8,128)}, f32[2,256,128]{2,1,0:T(8,128)S(1)}, u32[]{:S(2)}, u32[]{:S(2)}) collective-permute-start(f32[2,256,128]{2,1,0:T(8,128)} %get-tuple-element.152), channel_id=1, source_target_pairs={{0,4},{2,6},{4,0},{6,2},{8,12},{10,14},{12,8},{14,10},{16,20},{18,... | collective-permute-start | bytes 786440 | tf_op jit(solution)/shard_map/ppermute | solution.py:390
  228.7 14.6 %collective-permute-start.40 = (f32[256,384]{1,0:T(8,128)S(1)}, f32[256,384]{1,0:T(8,128)S(1)}, u32[]{:S(2)}, u32[]{:S(2)}) collective-permute-start(f32[256,384]{1,0:T(8,128)S(1)} %get-tuple-element.188), channel_id=1, source_target_pairs={{0,4},{2,6},{4,0},{6,2},{8,12},{10,14},{12,8},{14,10},{16,20},{18,... | collective-permute-start | bytes 1179656 | tf_op jit(solution)/shard_map/ppermute | solution.py:265
  229.2 14.0 %collective-permute-start.41 = (f32[256,384]{1,0:T(8,128)S(1)}, f32[256,384]{1,0:T(8,128)S(1)}, u32[]{:S(2)}, u32[]{:S(2)}) collective-permute-start(f32[256,384]{1,0:T(8,128)S(1)} %get-tuple-element.187), channel_id=1, source_target_pairs={{0,2},{2,0},{4,6},{6,4},{8,10},{10,8},{12,14},{14,12},{16,18},{18,... | collective-permute-start | bytes 1179656 | tf_op jit(solution)/shard_map/ppermute | solution.py:265
  243.4 17.0 %collective-permute-start.44 = (f32[512,384]{1,0:T(8,128)S(1)}, f32[512,384]{1,0:T(8,128)S(1)}, u32[]{:S(2)}, u32[]{:S(2)}) collective-permute-start(f32[512,384]{1,0:T(8,128)S(1)} %pad_maximum_fusion.2), channel_id=1, source_target_pairs={{0,4},{2,6},{4,0},{6,2},{8,12},{10,14},{12,8},{14,10},{16,20},{18,... | collective-permute-start | bytes 2359304 | tf_op jit(solution)/shard_map/ppermute | solution.py:265
  244.7 16.7 %collective-permute-start.43 = (f32[512,384]{1,0:T(8,128)S(1)}, f32[512,384]{1,0:T(8,128)S(1)}, u32[]{:S(2)}, u32[]{:S(2)}) collective-permute-start(f32[512,384]{1,0:T(8,128)S(1)} %pad_maximum_fusion.1), channel_id=1, source_target_pairs={{0,2},{2,0},{4,6},{6,4},{8,10},{10,8},{12,14},{14,12},{16,18},{18,... | collective-permute-start | bytes 2359304 | tf_op jit(solution)/shard_map/ppermute | solution.py:265
  (92 other events, 1000.8 us)
